TPU v7x, 512 devices: a whole 4x8x8 slice. The times are simulated.
512 devices in a mesh: gx: 8 (over z), gy: 8 (over y), gz: 8 (over x, core).
Axes of the slice: x: 4, y: 8, z: 8, core: 2. Of those that a mesh axis runs over, the one named last changes fastest.
Arguments:
- panel_in: bfloat16 [32, 64, 64, 1024], P(None, 'gx', 'gy', 'gz'), may hold values from -9 to 9
- prior_modes: bfloat16 [64, 64, 64, 1024], P(None, 'gx', 'gy', 'gz'), may hold values from -9 to 9, as said below
- stiffness: bfloat16 [64, 64, 1024], P('gx', 'gy', 'gz'), may hold values from 0.5 to 4
- mass_shift: bfloat16 [64, 64, 1024], P('gx', 'gy', 'gz'), may hold values from 2 to 16
Outputs:
- filtered_basis: bfloat16 [32, 64, 64, 1024], P(None, 'gx', 'gy', 'gz')
- upper_factor: float32 [32, 32], replicated
Inputs may be any that keep to these rules, and one draw needn't show every extreme that they name: `prior_modes`: orthonormal under the sum over nodes of products divided by 4194304.
All inputs are finite; a program needn't handle non-finite values.
Results may differ from a plain program's by a relative error of at most 0.0089.
The roundings to bfloat16 on the way count: a program that leaves them out, or rounds other values in their place, can miss the bound.
Values may be sent and summed in bfloat16 or wider, within the bound.
A program may use at most 128 MiB of HBM per device.

v0:
```python
import jax
import jax.numpy as jnp
import numpy as np
from jax import lax
from jax.sharding import PartitionSpec as P

filter_center = 10.0
filter_half = 12.0


def padded(cells, sides, width):
    for axis, dim in sides:
        count = lax.axis_size(axis)
        ends = count - 1
        head = lax.slice_in_dim(cells, 0, width, axis=dim)
        tail = lax.slice_in_dim(cells, cells.shape[dim] - width, cells.shape[dim], axis=dim)
        cells = jnp.concatenate(
            [
                lax.ppermute(tail, axis, [(i, (i + 1) % count) for i in range(ends)]),
                cells,
                lax.ppermute(head, axis, [((i + 1) % count, i) for i in range(ends)]),
            ],
            axis=dim,
        )
    return cells


def lobatto_tables():
    points = np.array([-1.0, -np.sqrt(3.0 / 7.0), 0.0, np.sqrt(3.0 / 7.0), 1.0])
    weights = np.array([0.1, 49.0 / 90.0, 32.0 / 45.0, 49.0 / 90.0, 0.1])
    scales = np.array(
        [np.prod([points[i] - points[k] for k in range(5) if k != i]) for i in range(5)]
    )
    derivative = np.zeros((5, 5))
    for i in range(5):
        for j in range(5):
            if j != i:
                derivative[i, j] = scales[i] / scales[j] / (points[i] - points[j])
        derivative[i, i] = -np.sum(derivative[i])
    return (derivative, weights)


def element_tables(length, offset, extent):
    derivative, weights = lobatto_tables()
    elements = (length - 1) // 4
    grad_table = np.zeros((5 * elements, length))
    pick_table = np.zeros((5 * elements, length))
    node_w = np.zeros(length)
    for m in range(elements):
        grad_table[5 * m : 5 * m + 5, 4 * m : 4 * m + 5] = derivative
        pick_table[5 * m : 5 * m + 5, 4 * m : 4 * m + 5] = np.eye(5)
        node_w[4 * m : 4 * m + 5] += weights
    grad_full = jnp.asarray(grad_table, jnp.float32).astype(jnp.bfloat16)
    grad_own = jnp.asarray(grad_table[:, offset : offset + extent], jnp.float32).astype(
        jnp.bfloat16
    )
    pick_full = jnp.asarray(pick_table, jnp.float32).astype(jnp.bfloat16)
    point_w = jnp.asarray(np.tile(weights, elements), jnp.float32)
    node_own = jnp.asarray(node_w[offset : offset + extent], jnp.float32)
    return (grad_full, grad_own, pick_full, point_w, node_own)


def operate(fields, stiff_field, mass_field, halo_width, keep_width):
    offset = halo_width - keep_width
    extents = [fields.shape[k + 1] - 2 * offset for k in range(3)]
    grad_x, own_x, pick_x, point_x, node_x = element_tables(fields.shape[1], offset, extents[0])
    grad_y, own_y, pick_y, point_y, node_y = element_tables(fields.shape[2], offset, extents[1])
    grad_z, own_z, pick_z, point_z, node_z = element_tables(fields.shape[3], offset, extents[2])
    span_x = slice(offset, offset + extents[0])
    span_y = slice(offset, offset + extents[1])
    span_z = slice(offset, offset + extents[2])
    slopes = jnp.einsum(
        "pa,vayz->vpyz", grad_x, fields[:, :, span_y, span_z], preferred_element_type=jnp.float32
    )
    kappas = jnp.einsum(
        "pa,ayz->pyz", pick_x, stiff_field[:, span_y, span_z], preferred_element_type=jnp.float32
    )
    factor = point_x[:, None, None] * kappas * node_y[None, :, None] * node_z[None, None, :]
    result = jnp.einsum(
        "pa,vpyz->vayz",
        own_x,
        (slopes * factor).astype(jnp.bfloat16),
        preferred_element_type=jnp.float32,
    )
    slopes = jnp.einsum(
        "pb,vxbz->vxpz", grad_y, fields[:, span_x, :, span_z], preferred_element_type=jnp.float32
    )
    kappas = jnp.einsum(
        "pb,xbz->xpz", pick_y, stiff_field[span_x, :, span_z], preferred_element_type=jnp.float32
    )
    factor = point_y[None, :, None] * kappas * node_x[:, None, None] * node_z[None, None, :]
    result = result + jnp.einsum(
        "pb,vxpz->vxbz",
        own_y,
        (slopes * factor).astype(jnp.bfloat16),
        preferred_element_type=jnp.float32,
    )
    slopes = jnp.einsum(
        "pc,vxyc->vxyp", grad_z, fields[:, span_x, span_y, :], preferred_element_type=jnp.float32
    )
    kappas = jnp.einsum(
        "pc,xyc->xyp", pick_z, stiff_field[span_x, span_y, :], preferred_element_type=jnp.float32
    )
    factor = point_z[None, None, :] * kappas * node_x[:, None, None] * node_y[None, :, None]
    result = result + jnp.einsum(
        "pc,vxyp->vxyc",
        own_z,
        (slopes * factor).astype(jnp.bfloat16),
        preferred_element_type=jnp.float32,
    )
    volume = node_x[:, None, None] * node_y[None, :, None] * node_z[None, None, :]
    mass_term = (
        volume
        * mass_field[span_x, span_y, span_z].astype(jnp.float32)
        * fields[:, span_x, span_y, span_z].astype(jnp.float32)
    )
    return result - mass_term


def on_device(panel_in, prior_modes, stiffness, mass_shift):
    vectors = panel_in.shape[0]
    extents = panel_in.shape[1:]
    nodes_total = (
        extents[0]
        * extents[1]
        * extents[2]
        * lax.axis_size("gx")
        * lax.axis_size("gy")
        * lax.axis_size("gz")
    )
    joined = jnp.concatenate([panel_in, stiffness[None], mass_shift[None]], axis=0)
    near_rim = padded(joined, (("gx", 1), ("gy", 2), ("gz", 3)), 3)
    stiff_near = near_rim[vectors]
    mass_near = near_rim[vectors + 1]
    first_image = operate(near_rim[:vectors], stiff_near, mass_near, 3, 0)
    filtered_one = (
        (first_image - filter_center * panel_in.astype(jnp.float32)) / filter_half
    ).astype(jnp.bfloat16)
    around_rim = padded(filtered_one, (("gx", 1), ("gy", 2), ("gz", 3)), 3)
    second_image = operate(around_rim, stiff_near, mass_near, 3, 0)
    owned_one = lax.optimization_barrier(filtered_one).astype(jnp.float32)
    filtered = (
        2.0 * (second_image - filter_center * owned_one) / filter_half
        - panel_in.astype(jnp.float32)
    ).astype(jnp.bfloat16)
    flat_y = filtered.reshape(vectors, -1)
    flat_p = prior_modes.reshape(prior_modes.shape[0], -1)
    projections = (
        lax.psum(jnp.dot(flat_p, flat_y.T, preferred_element_type=jnp.float32), ("gx", "gy", "gz"))
        / nodes_total
    )
    coeffs = projections.astype(jnp.bfloat16)
    residual = flat_y.astype(jnp.float32) - jnp.dot(
        coeffs.T, flat_p, preferred_element_type=jnp.float32
    )
    gram_matrix = (
        lax.psum(jnp.dot(residual, residual.T, precision=lax.Precision.HIGHEST), ("gx", "gy", "gz"))
        / nodes_total
    )
    lower_factor = jnp.linalg.cholesky(gram_matrix)
    inverse = jax.scipy.linalg.solve_triangular(
        lower_factor, jnp.eye(vectors, dtype=jnp.float32), lower=True
    )
    row_block = jnp.dot(inverse, residual, precision=lax.Precision.HIGHEST)
    return (row_block.reshape(panel_in.shape).astype(jnp.bfloat16), lower_factor.T)


def solution(mesh):
    placed = (
        P(None, "gx", "gy", "gz"),
        P(None, "gx", "gy", "gz"),
        P("gx", "gy", "gz"),
        P("gx", "gy", "gz"),
    )
    return jax.shard_map(
        on_device,
        mesh=mesh,
        in_specs=placed,
        out_specs=(P(None, "gx", "gy", "gz"), P()),
        check_vma=False,
    )
```

profile of v0, /device:TPU:1, one launch (start us, length us, event | category | flops | bytes accessed | tf_op | source)
XLA Modules:
  0.0 362.1 jit_solution(17603899345347308306)
XLA Ops:
  2.8 4.8 %collective-permute-start = (bf16[34,3,8,128]{3,1,2,0:T(4,128)(2,1)S(1)}, bf16[34,3,8,128]{3,1,2,0:T(4,128)(2,1)S(1)}, u32[]{:S(2)}, u32[]{:S(2)}) collective-permute-start(bf16[34,3,8,128]{3,1,2,0:T(4,128)(2,1)S(1)} %get-tuple-element.18), channel_id=1, source_target_pairs={{0,64},{64,128},{128,192},{192,256},{256,320},{320,384},{384,448},... | collective-permute-start | bytes 626696 | tf_op jit(solution)/shard_map/ppermute | solution.py:19
  7.6 1.3 collective-permute-start.1
  8.9 2.2 collective-permute-done
  11.1 4.5 %collective-permute-done.1 = bf16[34,3,8,128]{3,1,2,0:T(4,128)(2,1)S(1)} collective-permute-done((bf16[34,3,8,128]{3,1,2,0:T(4,128)(2,1)S(1)}, bf16[34,3,8,128]{3,1,2,0:T(4,128)(2,1)S(1)}, u32[]{:S(2)}, u32[]{:S(2)}) %collective-permute-start.1) | collective-permute-done | bytes 208928 | tf_op jit(solution)/shard_map/ppermute | solution.py:21
  16.0 5.4 %collective-permute-start.2 = (bf16[34,14,3,128]{3,1,2,0:T(8,128)(2,1)S(1)}, bf16[34,14,3,128]{3,1,2,0:T(8,128)(2,1)S(1)}, u32[]{:S(2)}, u32[]{:S(2)}) collective-permute-start(bf16[34,14,3,128]{3,1,2,0:T(8,128)(2,1)S(1)} %get-tuple-element.14), channel_id=1, source_target_pairs={{0,8},{8,16},{16,24},{24,32},{32,40},{40,48},{48,56},{1,9},{9,17},... | collective-permute-start | bytes 1096712 | tf_op jit(solution)/shard_map/ppermute | solution.py:19
  21.4 1.3 collective-permute-start.3
  22.7 6.0 %collective-permute-done.2 = bf16[34,14,3,128]{3,1,2,0:T(8,128)(2,1)S(1)} collective-permute-done((bf16[34,14,3,128]{3,1,2,0:T(8,128)(2,1)S(1)}, bf16[34,14,3,128]{3,1,2,0:T(8,128)(2,1)S(1)}, u32[]{:S(2)}, u32[]{:S(2)}) %collective-permute-start.2) | collective-permute-done | bytes 365600 | tf_op jit(solution)/shard_map/ppermute | solution.py:19
  28.8 3.9 %collective-permute-done.3 = bf16[34,14,3,128]{3,1,2,0:T(8,128)(2,1)S(1)} collective-permute-done((bf16[34,14,3,128]{3,1,2,0:T(8,128)(2,1)S(1)}, bf16[34,14,3,128]{3,1,2,0:T(8,128)(2,1)S(1)}, u32[]{:S(2)}, u32[]{:S(2)}) %collective-permute-start.3) | collective-permute-done | bytes 365600 | tf_op jit(solution)/shard_map/ppermute | solution.py:21
  33.4 1.9 pad_maximum_fusion.1
  35.3 2.8 fusion.90
  38.0 4.0 %copy.66 = bf16[34,14,14,3]{0,2,3,1:T(8,128)(2,1)} copy(bf16[34,14,14,3]{3,1,2,0:T(8,128)(2,1)} %get-tuple-element.10) | data formatting | bytes 79968 | tf_op jit(solution)/shard_map/slice | solution.py:16
  42.0 3.9 %copy.67 = bf16[34,14,14,3]{0,2,3,1:T(8,128)(2,1)} copy(bf16[34,14,14,3]{3,1,2,0:T(8,128)(2,1)} %get-tuple-element.11) | data formatting | bytes 79968 | tf_op jit(solution)/shard_map/slice | solution.py:15
  45.9 4.6 %collective-permute-start.5 = (bf16[34,14,14,3]{0,2,3,1:T(8,128)(2,1)}, bf16[34,14,14,3]{0,2,3,1:T(8,128)(2,1)}, u32[]{:S(2)}, u32[]{:S(2)}) collective-permute-start(bf16[34,14,14,3]{0,2,3,1:T(8,128)(2,1)} %copy.67), channel_id=1, source_target_pairs={{1,0},{2,1},{3,2},{4,3},{5,4},{6,5},{7,6},{9,8},{10,9},{11,10},{12... | collective-permute-start | bytes 119960 | tf_op jit(solution)/shard_map/ppermute | solution.py:21
  50.6 3.2 collective-permute-start.4
  54.1 2.1 collective-permute-done.4
  56.2 5.2 %copy.68 = bf16[34,14,14,3]{3,1,2,0:T(8,128)(2,1)S(1)} copy(bf16[34,14,14,3]{0,2,3,1:T(8,128)(2,1)} %collective-permute-done.4) | data formatting | bytes 79968 | tf_op jit(solution)/shard_map/ppermute | solution.py:19
  61.5 3.7 %copy.69 = bf16[34,14,14,3]{3,1,2,0:T(8,128)(2,1)} copy(bf16[34,14,14,3]{0,2,3,1:T(8,128)(2,1)} %collective-permute-done.5) | data formatting | bytes 79968 | tf_op jit(solution)/shard_map/ppermute | solution.py:21
  65.1 12.2 %pad_maximum_fusion = bf16[34,14,14,134]{3,1,2,0:T(8,128)(2,1)S(1)} fusion(bf16[34,14,14,3]{3,1,2,0:T(8,128)(2,1)} %copy.69, bf16[34,14,3,128]{3,1,2,0:T(8,128)(2,1)} %copy-done.5, bf16[34,3,8,128]{3,1,2,0:T(4,128)(2,1)} %copy-done.2, bf16[1,8,8,128]{3,1,2,0:T(8,128)(2,1)S(1)} %get-tuple-element.24, bf16[1,8,8,128]{3,1,2,0:T(8,128)(2,1)S(1)} %get-tuple-element.25, ...), kind=kLoop, calls=%fused_computation.2 | loop fusion | flops 16073568 | bytes 3571904 | tf_op jit(solution)/shard_map/concatenate | solution.py:17
  79.8 1.4 fusion.63
  81.2 1.5 fusion.7
  82.7 2.6 fusion.20
  85.6 4.0 %collective-permute-start.6 = (bf16[32,3,8,128]{3,1,2,0:T(4,128)(2,1)S(1)}, bf16[32,3,8,128]{3,1,2,0:T(4,128)(2,1)S(1)}, u32[]{:S(2)}, u32[]{:S(2)}) collective-permute-start(bf16[32,3,8,128]{3,1,2,0:T(4,128)(2,1)S(1)} %get-tuple-element.20), channel_id=1, source_target_pairs={{0,64},{64,128},{128,192},{192,256},{256,320},{320,384},{384,448},... | collective-permute-start | bytes 589832 | tf_op jit(solution)/shard_map/ppermute | solution.py:19
  89.6 1.3 collective-permute-start.7
  90.9 3.4 collective-permute-done.6
  94.3 5.7 %collective-permute-done.7 = bf16[32,3,8,128]{3,1,2,0:T(4,128)(2,1)S(1)} collective-permute-done((bf16[32,3,8,128]{3,1,2,0:T(4,128)(2,1)S(1)}, bf16[32,3,8,128]{3,1,2,0:T(4,128)(2,1)S(1)}, u32[]{:S(2)}, u32[]{:S(2)}) %collective-permute-start.7) | collective-permute-done | bytes 196640 | tf_op jit(solution)/shard_map/ppermute | solution.py:21
  100.4 3.2 collective-permute-start.8
  103.6 1.5 collective-permute-start.9
  105.1 7.0 %collective-permute-done.8 = bf16[32,14,3,128]{3,1,2,0:T(8,128)(2,1)S(1)} collective-permute-done((bf16[32,14,3,128]{3,1,2,0:T(8,128)(2,1)S(1)}, bf16[32,14,3,128]{3,1,2,0:T(8,128)(2,1)S(1)}, u32[]{:S(2)}, u32[]{:S(2)}) %collective-permute-start.8) | collective-permute-done | bytes 344096 | tf_op jit(solution)/shard_map/ppermute | solution.py:19
  112.2 4.7 %collective-permute-done.9 = bf16[32,14,3,128]{3,1,2,0:T(8,128)(2,1)S(1)} collective-permute-done((bf16[32,14,3,128]{3,1,2,0:T(8,128)(2,1)S(1)}, bf16[32,14,3,128]{3,1,2,0:T(8,128)(2,1)S(1)}, u32[]{:S(2)}, u32[]{:S(2)}) %collective-permute-start.9) | collective-permute-done | bytes 344096 | tf_op jit(solution)/shard_map/ppermute | solution.py:21
  117.7 1.3 slice.134
  118.9 2.1 fusion.91
  121.0 3.8 %copy.79 = bf16[32,14,14,3]{0,2,3,1:T(8,128)(2,1)} copy(bf16[32,14,14,3]{3,1,2,0:T(8,128)(2,1)} %get-tuple-element.12) | data formatting | bytes 75264 | tf_op jit(solution)/shard_map/slice | solution.py:16
  124.8 3.5 copy.80
  128.3 2.3 collective-permute-start.11
  130.5 3.5 collective-permute-start.10
  134.0 2.7 fusion.11
  136.8 4.8 %copy.81 = bf16[32,14,14,3]{3,1,2,0:T(8,128)(2,1)S(1)} copy(bf16[32,14,14,3]{0,2,3,1:T(8,128)(2,1)} %collective-permute-done.10) | data formatting | bytes 75264 | tf_op jit(solution)/shard_map/ppermute | solution.py:19
  141.5 3.6 copy.82
  145.1 2.6 pad_maximum_fusion.3
  148.2 1.4 fusion.61
  149.6 3.4 fusion.21
  153.0 1.2 copy.85
  154.2 2.2 convolution_bitcast_fusion
  156.4 98.5 %psum.14 = f32[64,32]{0,1:T(8,128)S(1)} all-reduce(f32[64,32]{0,1:T(8,128)S(1)} %convolution_bitcast_fusion), channel_id=1, replica_groups=mesh['gx'=8,'gy'=8,'gz'=8] {'gx','gy','gz'}, use_global_device_ids=true, to_apply=%region_0.0 | all-reduce | flops 2048 | bytes 16384 | tf_op jit(solution)/shard_map/psum | solution.py:149
  254.9 1.3 convolution_subtract_fusion
  257.1 95.4 %psum.15 = f32[32,32]{0,1:T(8,128)S(1)} all-reduce(f32[32,32]{0,1:T(8,128)S(1)} %fusion.94), channel_id=1, replica_groups=mesh['gx'=8,'gy'=8,'gz'=8] {'gx','gy','gz'}, use_global_device_ids=true, to_apply=%region_1.0 | all-reduce | flops 1024 | bytes 8192 | tf_op jit(solution)/shard_map/psum | solution.py:157
  352.6 2.9 cholesky.17
  357.5 2.4 custom-call.7
  (86 shorter events, 13.1 us)
Async XLA Ops:
  2.8 8.3 %collective-permute-start = (bf16[34,3,8,128]{3,1,2,0:T(4,128)(2,1)S(1)}, bf16[34,3,8,128]{3,1,2,0:T(4,128)(2,1)S(1)}, u32[]{:S(2)}, u32[]{:S(2)}) collective-permute-start(bf16[34,3,8,128]{3,1,2,0:T(4,128)(2,1)S(1)} %get-tuple-element.18), channel_id=1, source_target_pairs={{0,64},{64,128},{128,192},{192,256},{256,320},{320,384},{384,448},... | collective-permute-start | bytes 626696 | tf_op jit(solution)/shard_map/ppermute | solution.py:19
  7.6 7.9 %collective-permute-start.1 = (bf16[34,3,8,128]{3,1,2,0:T(4,128)(2,1)S(1)}, bf16[34,3,8,128]{3,1,2,0:T(4,128)(2,1)S(1)}, u32[]{:S(2)}, u32[]{:S(2)}) collective-permute-start(bf16[34,3,8,128]{3,1,2,0:T(4,128)(2,1)S(1)} %get-tuple-element.19), channel_id=1, source_target_pairs={{64,0},{128,64},{192,128},{256,192},{320,256},{384,320},{448,384},... | collective-permute-start | bytes 626696 | tf_op jit(solution)/shard_map/ppermute | solution.py:21
  11.1 21.5 %copy-start = (bf16[34,3,8,128]{3,1,2,0:T(4,128)(2,1)}, bf16[34,3,8,128]{3,1,2,0:T(4,128)(2,1)S(1)}, u32[]{:S(2)}) copy-start(bf16[34,3,8,128]{3,1,2,0:T(4,128)(2,1)S(1)} %collective-permute-done) | copy-start | bytes 626692
  15.6 17.1 %copy-start.2 = (bf16[34,3,8,128]{3,1,2,0:T(4,128)(2,1)}, bf16[34,3,8,128]{3,1,2,0:T(4,128)(2,1)S(1)}, u32[]{:S(2)}) copy-start(bf16[34,3,8,128]{3,1,2,0:T(4,128)(2,1)S(1)} %collective-permute-done.1) | copy-start | bytes 626692
  16.0 12.7 %collective-permute-start.2 = (bf16[34,14,3,128]{3,1,2,0:T(8,128)(2,1)S(1)}, bf16[34,14,3,128]{3,1,2,0:T(8,128)(2,1)S(1)}, u32[]{:S(2)}, u32[]{:S(2)}) collective-permute-start(bf16[34,14,3,128]{3,1,2,0:T(8,128)(2,1)S(1)} %get-tuple-element.14), channel_id=1, source_target_pairs={{0,8},{8,16},{16,24},{24,32},{32,40},{40,48},{48,56},{1,9},{9,17},... | collective-permute-start | bytes 1096712 | tf_op jit(solution)/shard_map/ppermute | solution.py:19
  21.4 11.2 %collective-permute-start.3 = (bf16[34,14,3,128]{3,1,2,0:T(8,128)(2,1)S(1)}, bf16[34,14,3,128]{3,1,2,0:T(8,128)(2,1)S(1)}, u32[]{:S(2)}, u32[]{:S(2)}) collective-permute-start(bf16[34,14,3,128]{3,1,2,0:T(8,128)(2,1)S(1)} %get-tuple-element.15), channel_id=1, source_target_pairs={{8,0},{16,8},{24,16},{32,24},{40,32},{48,40},{56,48},{9,1},{17,9},... | collective-permute-start | bytes 1096712 | tf_op jit(solution)/shard_map/ppermute | solution.py:21
  28.8 3.9 %copy-start.4 = (bf16[34,14,3,128]{3,1,2,0:T(8,128)(2,1)}, bf16[34,14,3,128]{3,1,2,0:T(8,128)(2,1)S(1)}, u32[]{:S(2)}) copy-start(bf16[34,14,3,128]{3,1,2,0:T(8,128)(2,1)S(1)} %collective-permute-done.2) | copy-start | bytes 1096708
  32.6 0.8 copy-start.5
  38.0 15.8 %copy-start.17 = (f32[8]{0:T(128)S(1)}, f32[8]{0:T(128)}, u32[]{:S(2)}) copy-start(f32[8]{0:T(128)} %constant.81.clone) | copy-start | bytes 100
  45.9 15.6 %collective-permute-start.5 = (bf16[34,14,14,3]{0,2,3,1:T(8,128)(2,1)}, bf16[34,14,14,3]{0,2,3,1:T(8,128)(2,1)}, u32[]{:S(2)}, u32[]{:S(2)}) collective-permute-start(bf16[34,14,14,3]{0,2,3,1:T(8,128)(2,1)} %copy.67), channel_id=1, source_target_pairs={{1,0},{2,1},{3,2},{4,3},{5,4},{6,5},{7,6},{9,8},{10,9},{11,10},{12... | collective-permute-start | bytes 119960 | tf_op jit(solution)/shard_map/ppermute | solution.py:21
  50.6 5.7 %collective-permute-start.4 = (bf16[34,14,14,3]{0,2,3,1:T(8,128)(2,1)}, bf16[34,14,14,3]{0,2,3,1:T(8,128)(2,1)}, u32[]{:S(2)}, u32[]{:S(2)}) collective-permute-start(bf16[34,14,14,3]{0,2,3,1:T(8,128)(2,1)} %copy.66), channel_id=1, source_target_pairs={{0,1},{1,2},{2,3},{3,4},{4,5},{5,6},{6,7},{8,9},{9,10},{10,11},{11... | collective-permute-start | bytes 119960 | tf_op jit(solution)/shard_map/ppermute | solution.py:19
  77.4 0.7 copy-start.19
  77.4 0.7 copy-start.21
  77.4 0.7 copy-start.22
  77.4 1.1 copy-start.10
  77.4 1.1 copy-start.23
  77.4 1.9 copy-start.24
  77.5 2.3 copy-start.9
  78.3 4.5 %copy-start.11 = (f32[15,8,128]{2,0,1:T(8,128)}, f32[15,8,128]{2,0,1:T(8,128)S(1)}, u32[]{:S(2)}) copy-start(f32[15,8,128]{2,0,1:T(8,128)S(1)} %fusion.30) | copy-start | bytes 184324
  78.5 4.2 %copy-start.15 = (f32[8,8,128]{2,0,1:T(8,128)}, f32[8,8,128]{2,0,1:T(8,128)S(1)}, u32[]{:S(2)}) copy-start(f32[8,8,128]{2,0,1:T(8,128)S(1)} %convert_multiply_fusion.2) | copy-start | bytes 98308
  78.7 0.6 copy-start.13
  79.3 1.9 copy-start.18
  79.3 1.9 copy-start.20
  79.8 3.0 copy-start.1
  79.8 3.0 copy-start.3
  85.6 8.7 %collective-permute-start.6 = (bf16[32,3,8,128]{3,1,2,0:T(4,128)(2,1)S(1)}, bf16[32,3,8,128]{3,1,2,0:T(4,128)(2,1)S(1)}, u32[]{:S(2)}, u32[]{:S(2)}) collective-permute-start(bf16[32,3,8,128]{3,1,2,0:T(4,128)(2,1)S(1)} %get-tuple-element.20), channel_id=1, source_target_pairs={{0,64},{64,128},{128,192},{192,256},{256,320},{320,384},{384,448},... | collective-permute-start | bytes 589832 | tf_op jit(solution)/shard_map/ppermute | solution.py:19
  89.6 10.3 %collective-permute-start.7 = (bf16[32,3,8,128]{3,1,2,0:T(4,128)(2,1)S(1)}, bf16[32,3,8,128]{3,1,2,0:T(4,128)(2,1)S(1)}, u32[]{:S(2)}, u32[]{:S(2)}) collective-permute-start(bf16[32,3,8,128]{3,1,2,0:T(4,128)(2,1)S(1)} %get-tuple-element.21), channel_id=1, source_target_pairs={{64,0},{128,64},{192,128},{256,192},{320,256},{384,320},{448,384},... | collective-permute-start | bytes 589832 | tf_op jit(solution)/shard_map/ppermute | solution.py:21
  100.4 11.8 %collective-permute-start.8 = (bf16[32,14,3,128]{3,1,2,0:T(8,128)(2,1)S(1)}, bf16[32,14,3,128]{3,1,2,0:T(8,128)(2,1)S(1)}, u32[]{:S(2)}, u32[]{:S(2)}) collective-permute-start(bf16[32,14,3,128]{3,1,2,0:T(8,128)(2,1)S(1)} %get-tuple-element.16), channel_id=1, source_target_pairs={{0,8},{8,16},{16,24},{24,32},{32,40},{40,48},{48,56},{1,9},{9,17},... | collective-permute-start | bytes 1032200 | tf_op jit(solution)/shard_map/ppermute | solution.py:19
  103.6 13.3 %collective-permute-start.9 = (bf16[32,14,3,128]{3,1,2,0:T(8,128)(2,1)S(1)}, bf16[32,14,3,128]{3,1,2,0:T(8,128)(2,1)S(1)}, u32[]{:S(2)}, u32[]{:S(2)}) collective-permute-start(bf16[32,14,3,128]{3,1,2,0:T(8,128)(2,1)S(1)} %get-tuple-element.17), channel_id=1, source_target_pairs={{8,0},{16,8},{24,16},{32,24},{40,32},{48,40},{56,48},{9,1},{17,9},... | collective-permute-start | bytes 1032200 | tf_op jit(solution)/shard_map/ppermute | solution.py:21
  116.9 0.8 copy-start.6
  128.3 13.2 %collective-permute-start.11 = (bf16[32,14,14,3]{0,2,3,1:T(8,128)(2,1)}, bf16[32,14,14,3]{0,2,3,1:T(8,128)(2,1)}, u32[]{:S(2)}, u32[]{:S(2)}) collective-permute-start(bf16[32,14,14,3]{0,2,3,1:T(8,128)(2,1)} %copy.80), channel_id=1, source_target_pairs={{1,0},{2,1},{3,2},{4,3},{5,4},{6,5},{7,6},{9,8},{10,9},{11,10},{12... | collective-permute-start | bytes 112904 | tf_op jit(solution)/shard_map/ppermute | solution.py:21
  130.5 6.2 %collective-permute-start.10 = (bf16[32,14,14,3]{0,2,3,1:T(8,128)(2,1)}, bf16[32,14,14,3]{0,2,3,1:T(8,128)(2,1)}, u32[]{:S(2)}, u32[]{:S(2)}) collective-permute-start(bf16[32,14,14,3]{0,2,3,1:T(8,128)(2,1)} %copy.79), channel_id=1, source_target_pairs={{0,1},{1,2},{2,3},{3,4},{4,5},{5,6},{6,7},{8,9},{9,10},{10,11},{11... | collective-permute-start | bytes 112904 | tf_op jit(solution)/shard_map/ppermute | solution.py:19
  145.1 2.6 copy-start.14
  145.1 2.6 copy-start.25
  147.7 1.9 copy-start.8
  147.7 1.9 copy-start.12
  147.8 1.9 copy-start.16
  149.6 4.6 %copy-start.7 = (bf16[64,8,8,128]{3,2,1,0:T(8,128)(2,1)S(1)}, bf16[64,8,8,128]{3,2,1,0:T(8,128)(2,1)}, u32[]{:S(2)}) copy-start(bf16[64,8,8,128]{3,2,1,0:T(8,128)(2,1)} %param.35) | copy-start | bytes 3145732
where the time goes:
time: 363 us; the launch traced here: 362 us
  blocking collectives  194 us (53%)
  local copies, waits for them, and re-layouts  45.9 us (13%)
  waiting for transfers between devices  39.4 us (11%)
  starting transfers between devices  36.4 us (10%)
  other arithmetic  25.4 us (7%)
  matrix products  20.2 us (6%)
    psum x1, blocking collectives, on_device(): lax.psum(jnp.dot(flat_p, flat_y.T, preferred_element_type=jnp.float32), (...  98.5 us
    psum x1, blocking collectives, on_device(): lax.psum(jnp.dot(residual, residual.T, precision=lax.Precision.HIGHEST),...  95.4 us
    ppermute x6, starting transfers between devices, padded(): lax.ppermute(tail, axis, [(i, (i + 1) % count) for i in range(ends)])  24.1 us
    ppermute x6, waiting for transfers between devices, padded(): lax.ppermute(tail, axis, [(i, (i + 1) % count) for i in range(ends)])  20.7 us
    ppermute x6, waiting for transfers between devices, padded(): lax.ppermute(head, axis, [((i + 1) % count, i) for i in range(ends)])  18.7 us
    concatenate x4, other arithmetic, padded(): jnp.concatenate([lax.ppermute(tail, axis, [(i, (i + 1) % count) for i in...  17.5 us
    slice x6, local copies, waits for them, and re-layouts, padded(): lax.slice_in_dim(cells, cells.shape[dim] - width, cells.shape[dim], axis=...  12.9 us
    ppermute x6, starting transfers between devices, padded(): lax.ppermute(head, axis, [((i + 1) % count, i) for i in range(ends)])  12.3 us
  transfers between devices with their start and end apart: 12, of which 9 were waited for; matrix products, arithmetic and copies ran while one was open for 4% of the time, Pallas kernels for 0%

commit v1 on v0

v1 whole, which is shorter than its diff:
```python
import functools

import jax
import jax.numpy as jnp
import ml_dtypes
import numpy as np
from jax import lax
from jax.experimental import pallas as pl
from jax.experimental.pallas import tpu as pltpu
from jax.sharding import PartitionSpec as P

filter_center = 10.0
filter_half = 12.0

MESH = pl.DeviceIdType.MESH
BF16 = jnp.bfloat16
F32 = jnp.float32
VECS = 32
PRIOR = 64
SIDE = 8
ROWS = SIDE * SIDE
LANES = 128
CHUNK = 8
CHUNKS = VECS // CHUNK
PAIRS = CHUNK // 2
SLOT = LANES // CHUNK
POINTS_Z = 5 * (LANES // 4 + 1)


def lobatto_tables():
    points = np.array([-1.0, -np.sqrt(3.0 / 7.0), 0.0, np.sqrt(3.0 / 7.0), 1.0])
    weights = np.array([0.1, 49.0 / 90.0, 32.0 / 45.0, 49.0 / 90.0, 0.1])
    scales = np.array(
        [np.prod([points[i] - points[k] for k in range(5) if k != i]) for i in range(5)]
    )
    derivative = np.zeros((5, 5))
    for i in range(5):
        for j in range(5):
            if j != i:
                derivative[i, j] = scales[i] / scales[j] / (points[i] - points[j])
        derivative[i, i] = -np.sum(derivative[i])
    return (derivative, weights)


def node_weight(count):
    weights = lobatto_tables()[1]
    per_node = [weights[3], weights[4] + weights[0], weights[1], weights[2]]
    return np.array([per_node[i % 4] for i in range(count)])


HIGH_X, HIGH_Y, LOW_X, LOW_Y = 64, 80, 96, 144
BLOCK = 256


def field_row(x, y, parity):
    if x < 0:
        return LOW_X + 24 * parity + (x + 3) * SIDE + y
    if y < 0:
        return LOW_Y + 24 * parity + (y + 3) * SIDE + x
    if x >= SIDE:
        return HIGH_X + (x - SIDE) * SIDE + y
    if y >= SIDE:
        return HIGH_Y + (y - SIDE) * SIDE + x
    return x * SIDE + y


def stiff_row(x, y):
    if x < 0:
        return ROWS + (x + SIDE) * SIDE + y
    if x >= SIDE:
        return 2 * ROWS + (x - SIDE) * SIDE + y
    if y < 0:
        return 3 * ROWS + x * SIDE + y + SIDE
    if y >= SIDE:
        return 4 * ROWS + x * SIDE + y - SIDE
    return x * SIDE + y


STIFF_K = 384


def make_tables():
    derivative, weights = lobatto_tables()
    node_w = node_weight(SIDE)
    node_z = node_weight(LANES)
    grad = np.zeros((2, BLOCK, BLOCK))
    back = np.zeros((ROWS, BLOCK))
    pick = np.zeros((BLOCK, STIFF_K))
    scale = np.zeros((BLOCK, LANES))
    for m in range(3):
        for q in range(5):
            for t in range(SIDE):
                rx = (m * 5 + q) * SIDE + t
                ry = 120 + rx
                at = 4 * m - 3 + q
                pick[rx, stiff_row(at, t)] = 1
                pick[ry, stiff_row(t, at)] = 1
                scale[rx] = weights[q] * node_w[t] * node_z
                scale[ry] = weights[q] * node_w[t] * node_z
                for a in range(5):
                    node = 4 * m - 3 + a
                    for parity in range(2):
                        grad[parity, rx, field_row(node, t, parity)] = derivative[q, a]
                        grad[parity, ry, field_row(t, node, parity)] = derivative[q, a]
                    if 0 <= node < SIDE:
                        back[node * SIDE + t, rx] = derivative[q, a]
                        back[t * SIDE + node, ry] = derivative[q, a]
    grad_z = np.zeros((2 * LANES, BLOCK))
    back_z = np.zeros((BLOCK, LANES))
    pick_z = np.zeros((3 * LANES, BLOCK))
    scale_z = np.zeros((ROWS, BLOCK))
    for m in range(LANES // 4 + 1):
        for q in range(5):
            col = 5 * m + q
            at = 4 * m - 3 + q
            source = at if 0 <= at < LANES else (2 * LANES + at if at < 0 else LANES + at)
            pick_z[source, col] = 1
            for t in range(ROWS):
                scale_z[t, col] = weights[q] * node_w[t // SIDE] * node_w[t % SIDE]
            for a in range(5):
                node = 4 * m - 3 + a
                row = node
                if node < 0:
                    row = LANES + node + 3
                elif node >= LANES:
                    row = LANES + 3 + node - LANES
                else:
                    back_z[col, node] = derivative[q, a]
                grad_z[row, col] = derivative[q, a]
    faces = np.zeros((128, 128))
    for half in range(2):
        for t in range(SIDE):
            for j in range(2):
                faces[16 * half + j * SIDE + t, 64 * half + t * SIDE + j] = 1
            for j in range(3):
                faces[32 + 24 * half + j * SIDE + t, 64 * half + (5 + j) * SIDE + t] = 1
                faces[80 + 24 * half + j * SIDE + t, 64 * half + t * SIDE + 5 + j] = 1
    ends = np.zeros((CHUNK * LANES, LANES))
    for j in range(CHUNK):
        for i in range(5):
            ends[j * LANES + (LANES - 3 + i) % LANES, j * SLOT + i] = 1
    volume = np.zeros((ROWS, LANES))
    for t in range(ROWS):
        volume[t] = node_w[t // SIDE] * node_w[t % SIDE] * node_z
    fold = np.zeros((VECS, VECS * SIDE))
    for v in range(VECS):
        fold[v, v * SIDE : (v + 1) * SIDE] = 1
    spread = np.zeros((2 * VECS * SIDE, 2 * VECS))
    for v in range(2 * VECS):
        spread[v * SIDE : (v + 1) * SIDE, v] = 1
    gather = np.zeros(((VECS + PRIOR) * SIDE, LANES))
    for u in range(VECS + PRIOR):
        gather[u * SIDE : (u + 1) * SIDE, u] = 1
    halves = [grad, back, pick, grad_z, back_z, pick_z, faces, ends, fold, spread, gather]
    singles = [scale, scale_z, volume]
    return [t.astype(np.float32).astype(ml_dtypes.bfloat16) for t in halves] + [
        t.astype(np.float32) for t in singles
    ]


def dot(a, b):
    return jnp.dot(a, b, preferred_element_type=F32)


def dot_nt(a, b, precision=None):
    return lax.dot_general(
        a, b, (((1,), (1,)), ((), ())), precision=precision, preferred_element_type=F32
    )


def split3(a):
    first = a.astype(BF16)
    rest = a - first.astype(F32)
    second = rest.astype(BF16)
    third = (rest - second.astype(F32)).astype(BF16)
    return first, second, third


def side(shape, dim):
    return lax.broadcasted_iota(jnp.int32, shape, dim)


TABLES = 14


def kernel(sizes, nodes_total, *refs):
    panel, prior, stiff, mass = refs[:4]
    tables = refs[4 : 4 + TABLES]
    out, upper = refs[4 + TABLES : 6 + TABLES]
    scratch = refs[6 + TABLES :]
    held = scratch[:TABLES]
    grad, back, pick, grad_z, back_z, pick_z, faces, ends, fold, spread, gather = held[:11]
    scale, scale_z, volume = held[11:]
    (
        field,
        modes,
        stiff_own,
        mass_own,
        once,
        low_x_s,
        high_x_s,
        low_y_s,
        high_y_s,
        ends_s,
        low_x_r,
        high_x_r,
        low_y_r,
        high_y_r,
        low_z_r,
        high_z_r,
        stiff_r,
        factor,
        factor_z,
        shift,
        stack,
        total_s,
        scatter_r,
        sum_x,
        sum_y,
        gathered,
        result,
        load_sem,
        field_sem,
        out_sem,
        stiff_send,
        stiff_recv,
        face_send,
        face_recv,
        sum_send,
        sum_recv,
    ) = scratch[TABLES:]
    nx, ny, nz = sizes
    axes = ("gx", "gy", "gz")
    me = [lax.axis_index(a) for a in axes]

    def along(axis, step):
        return {axes[axis]: lax.rem(me[axis] + step + sizes[axis], sizes[axis])}

    field_loads = []
    for c in range(CHUNKS):
        part = pl.ds(c * CHUNK, CHUNK)
        load = pltpu.make_async_copy(panel.at[part], field.at[part], field_sem.at[c])
        load.start()
        field_loads.append(load)
    loads = []
    for k, (src, dst) in enumerate(
        [(stiff, stiff_own), (mass, mass_own), (prior, modes)] + list(zip(tables, held))
    ):
        load = pltpu.make_async_copy(src, dst, load_sem.at[k])
        load.start()
        loads.append(load)
    barrier = pltpu.get_barrier_semaphore()
    for axis in range(3):
        for step in range(1, sizes[axis]):
            pl.semaphore_signal(
                barrier, inc=1, device_id=along(axis, step), device_id_type=MESH
            )

    def pack(app, c, source):
        cells = [source[c * CHUNK + j] for j in range(CHUNK)]
        pairs = [
            jnp.concatenate([cells[2 * p], cells[2 * p + 1]], axis=1) for p in range(PAIRS)
        ]
        for p in range(PAIRS):
            high_x_s[app, c, 16 * p : 16 * p + 16] = pairs[p][:16]
        for q in range(PAIRS // 2):
            both = jnp.concatenate([pairs[2 * q], pairs[2 * q + 1]], axis=0)
            picked = dot(faces[...], both).astype(BF16)
            high_y_s[app, c, 32 * q : 32 * q + 32] = picked[:32]
            low_x_s[app, c, 48 * q : 48 * q + 48] = picked[32:80]
            low_y_s[app, c, 48 * q : 48 * q + 48] = picked[80:]
        ends_s[app, c] = dot(jnp.concatenate(cells, axis=1), ends[...]).astype(BF16)

    def face_copies(app, c):
        plan = [
            (low_x_s, low_x_r, 0, 1),
            (high_x_s, high_x_r, 0, -1),
            (low_y_s, low_y_r, 1, 1),
            (high_y_s, high_y_r, 1, -1),
            (ends_s, low_z_r, 2, 1),
            (ends_s, high_z_r, 2, -1),
        ]
        return [
            pltpu.make_async_remote_copy(
                src_ref=src.at[app, c],
                dst_ref=dst.at[app, c],
                send_sem=face_send.at[app, c, k],
                recv_sem=face_recv.at[app, c, k],
                device_id=along(axis, step),
                device_id_type=MESH,
            )
            for k, (src, dst, axis, step) in enumerate(plan)
        ]

    def stiff_copies():
        return [
            pltpu.make_async_remote_copy(
                src_ref=stiff_own,
                dst_ref=stiff_r.at[k],
                send_sem=stiff_send.at[k],
                recv_sem=stiff_recv.at[k],
                device_id=along(k // 2, 1 - 2 * (k % 2)),
                device_id_type=MESH,
            )
            for k in range(6)
        ]

    for load in loads:
        load.wait()
    for load in field_loads:
        load.wait()

    @pl.loop(0, CHUNKS)
    def _(c):
        pack(0, c, field)

    pl.semaphore_wait(barrier, nx + ny + nz - 3)
    for copy in stiff_copies():
        copy.start()

    @pl.loop(0, CHUNKS)
    def _(c):
        for copy in face_copies(0, c):
            copy.start()

    first = [me[k] == 0 for k in range(3)]
    last = [me[k] == sizes[k] - 1 for k in range(3)]

    def outside(index, spans):
        cut = index < 0
        for low, high, missing in spans:
            cut = cut | ((index >= low) & (index < high) & missing)
        return cut

    col = side((BLOCK, BLOCK), 1)
    cut = outside(
        col,
        [
            (HIGH_X, HIGH_Y, last[0]),
            (HIGH_Y, LOW_X, last[1]),
            (LOW_X, LOW_Y, first[0]),
            (LOW_Y, LOW_Y + 48, first[1]),
        ],
    )
    for parity in range(2):
        grad[parity] = jnp.where(cut, 0.0, grad[parity].astype(F32)).astype(BF16)
    row = side((2 * LANES, BLOCK), 0)
    cut = outside(row, [(LANES, LANES + 3, first[2]), (LANES + 3, LANES + 5, last[2])])
    grad_z[...] = jnp.where(cut, 0.0, grad_z[...].astype(F32)).astype(BF16)
    col = side((BLOCK, STIFF_K), 1)
    cut = outside(
        col,
        [
            (ROWS, 2 * ROWS, first[0]),
            (2 * ROWS, 3 * ROWS, last[0]),
            (3 * ROWS, 4 * ROWS, first[1]),
            (4 * ROWS, 5 * ROWS, last[1]),
        ],
    )
    pick[...] = jnp.where(cut, 0.0, pick[...].astype(F32)).astype(BF16)
    row = side((3 * LANES, BLOCK), 0)
    cut = outside(row, [(LANES, 2 * LANES, first[2]), (2 * LANES, 3 * LANES, last[2])])
    pick_z[...] = jnp.where(cut, 0.0, pick_z[...].astype(F32)).astype(BF16)

    shift[...] = volume[...] * mass_own[...].astype(F32) + filter_center

    @pl.loop(0, PRIOR // 2)
    def _(p):
        one = modes[2 * p].astype(F32)
        two = modes[2 * p + 1].astype(F32)
        at = pl.ds(pl.multiple_of(VECS * SIDE + 16 * p, 16), 16)
        for x in range(SIDE):
            rows = slice(x * SIDE, (x + 1) * SIDE)
            stack[at, x * LANES : (x + 1) * LANES] = jnp.concatenate(
                [one[rows], two[rows]], axis=0
            ).astype(BF16)

    for copy in stiff_copies():
        copy.wait_recv()
    around = jnp.concatenate(
        [stiff_own[...]]
        + [stiff_r[k] for k in range(4)]
        + [jnp.zeros((STIFF_K - 5 * ROWS, LANES), BF16)],
        axis=0,
    )
    factor[...] = dot(pick[...], around) * scale[...]
    around = jnp.concatenate([stiff_own[...], stiff_r[4], stiff_r[5]], axis=1)
    factor_z[...] = dot(around, pick_z[...]) * scale_z[...]

    def operate(app, c, source, finish):
        slot = lax.rem(side((ROWS, LANES), 1), SLOT)
        joined = jnp.where(
            slot < 3, low_z_r[app, c].astype(F32), high_z_r[app, c].astype(F32)
        )
        factor_two = jnp.concatenate([factor[...], factor[...]], axis=1)
        factor_rows = jnp.concatenate([factor_z[...], factor_z[...]], axis=0)
        for p in range(PAIRS):
            q, parity = p // 2, p % 2
            cells = [source[c * CHUNK + 2 * p + h] for h in range(2)]
            rows = jnp.concatenate(
                [
                    jnp.concatenate(cells, axis=1),
                    high_x_r[app, c, 16 * p : 16 * p + 16],
                    high_y_r[app, c, 16 * p : 16 * p + 16],
                    low_x_r[app, c, 48 * q : 48 * q + 48],
                    low_y_r[app, c, 48 * q : 48 * q + 48],
                    jnp.zeros((BLOCK - 192, 2 * LANES), BF16),
                ],
                axis=0,
            )
            flux = (dot(grad[parity], rows) * factor_two).astype(BF16)
            image = dot(back[...], flux)
            lines = []
            for h in range(2):
                j = 2 * p + h
                rolled = pltpu.roll(joined, LANES - SLOT * j, 1) if j else joined
                lines.append(jnp.concatenate([cells[h], rolled.astype(BF16)], axis=1))
            flux_z = (dot(jnp.concatenate(lines, axis=0), grad_z[...]) * factor_rows).astype(
                BF16
            )
            image_z = dot(flux_z, back_z[...])
            moved = [
                image[:, h * LANES : (h + 1) * LANES]
                + image_z[h * ROWS : (h + 1) * ROWS]
                - shift[...] * cells[h].astype(F32)
                for h in range(2)
            ]
            finish(c, p, moved)

    def finish_one(c, p, moved):
        for h in range(2):
            once[c * CHUNK + 2 * p + h] = (moved[h] * (1.0 / filter_half)).astype(BF16)

    def finish_two(c, p, moved):
        done = [
            moved[h] * (2.0 / filter_half) - field[c * CHUNK + 2 * p + h].astype(F32)
            for h in range(2)
        ]
        at = pl.ds(pl.multiple_of(c * (CHUNK * SIDE) + 16 * p, 16), 16)
        for x in range(SIDE):
            rows = slice(x * SIDE, (x + 1) * SIDE)
            stack[at, x * LANES : (x + 1) * LANES] = jnp.concatenate(
                [done[0][rows], done[1][rows]], axis=0
            ).astype(BF16)

    @pl.loop(0, CHUNKS)
    def _(c):
        for copy in face_copies(0, c):
            copy.wait_recv()
        operate(0, c, field, finish_one)
        pack(1, c, once)
        for copy in face_copies(1, c):
            copy.start()

    @pl.loop(0, CHUNKS)
    def _(c):
        for copy in face_copies(1, c):
            copy.wait_recv()
        operate(1, c, once, finish_two)

    wide = VECS * SIDE
    tall = (VECS + PRIOR) * SIDE
    cross = dot_nt(stack[:wide], stack[...])
    same = lax.rem(side((wide, tall), 0), SIDE) == lax.rem(side((wide, tall), 1), SIDE)
    folded = sum(dot(fold[...], t) for t in split3(jnp.where(same, cross, 0.0)))
    sums = sum(dot(t, gather[...]) for t in split3(folded))

    share = VECS // nz

    def sum_copies(stage, axis, source, target):
        copies = []
        for step in range(1, sizes[axis]):
            to = lax.rem(me[axis] + step, sizes[axis])
            copies.append(
                pltpu.make_async_remote_copy(
                    src_ref=source(to),
                    dst_ref=target(step),
                    send_sem=sum_send.at[stage, step],
                    recv_sem=sum_recv.at[stage, step],
                    device_id={axes[axis]: to},
                    device_id_type=MESH,
                )
            )
        for copy in copies:
            copy.start()
        for copy in copies:
            copy.wait_recv()
        return copies

    for k in range(nz):
        total_s[k] = sums[k * share : (k + 1) * share]
    sent = sum_copies(0, 2, lambda to: total_s.at[to], lambda step: scatter_r.at[step])
    mine = total_s[me[2]]
    for step in range(1, nz):
        mine = mine + scatter_r[step]
    for stage, axis, slots in ((1, 0, sum_x), (2, 1, sum_y)):
        slots[me[axis]] = mine
        here = slots.at[me[axis]]
        sent += sum_copies(stage, axis, lambda to: here, lambda step: here)
        mine = slots[0]
        for k in range(1, sizes[axis]):
            mine = mine + slots[k]
    gathered[me[2]] = mine
    here = gathered.at[me[2]]
    sent += sum_copies(3, 2, lambda to: here, lambda step: here)
    sums = jnp.concatenate([gathered[k] for k in range(nz)], axis=0) * (1.0 / nodes_total)

    lane = side((VECS, LANES), 1)
    line = side((VECS, LANES), 0)
    proj = jnp.where((lane >= VECS) & (lane < VECS + PRIOR), sums, 0.0)
    coeffs = proj.astype(BF16).astype(F32)
    rest = proj - coeffs
    exact = lax.Precision.HIGHEST
    gram = sums[:, :VECS] - dot_nt(proj, proj, exact) + dot_nt(rest, rest, exact)
    solve = jnp.where(lane == line, 1.0, 0.0) - coeffs
    below = side((VECS, 1), 0)
    for k in range(VECS):
        ratio = jnp.where(below > k, gram[:, k : k + 1] / gram[k : k + 1, k : k + 1], 0.0)
        solve = solve - ratio * solve[k : k + 1]
        gram = gram - ratio * gram[k : k + 1]
    left = side((VECS, VECS), 0)
    right = side((VECS, VECS), 1)
    pivots = jnp.sum(jnp.where(left == right, gram, 0.0), axis=1, keepdims=True)
    inverse = 1.0 / jnp.sqrt(pivots)
    upper[...] = jnp.where(right >= left, gram * inverse, 0.0)
    solve = solve * inverse

    high = solve.astype(BF16)
    low = (solve - high.astype(F32)).astype(BF16)
    widened = dot_nt(jnp.concatenate([high, low], axis=0), gather[...]).astype(BF16)
    widened = dot(spread[...], widened)
    shape = (2 * wide, tall)
    same = lax.rem(side(shape, 0), SIDE) == lax.rem(side(shape, 1), SIDE)
    widened = jnp.where(same, widened, 0.0).astype(BF16)
    writes = []
    for x in range(0, SIDE, 2):
        block = dot(widened, stack[:, x * LANES : (x + 2) * LANES])
        block = block[:wide] + block[wide:]
        for v in range(VECS):
            rows = block[v * SIDE : (v + 1) * SIDE]
            result[v, x * SIDE : (x + 2) * SIDE] = jnp.concatenate(
                [rows[:, :LANES], rows[:, LANES:]], axis=0
            ).astype(BF16)
        part = pl.ds(x * SIDE, 2 * SIDE)
        write = pltpu.make_async_copy(
            result.at[:, part], out.at[:, part], out_sem.at[x // 2]
        )
        write.start()
        writes.append(write)

    for copy in sent + stiff_copies():
        copy.wait_send()

    @pl.loop(0, CHUNKS)
    def _(c):
        for app in range(2):
            for copy in face_copies(app, c):
                copy.wait_send()

    for write in writes:
        write.wait()


def on_device(sizes, nodes_total, panel_in, prior_modes, stiffness, mass_shift):
    nx, ny, nz = sizes
    share = VECS // nz
    tables = make_tables()
    low = (2, CHUNKS, 24 * PAIRS, 2 * LANES)
    high = (2, CHUNKS, 16 * PAIRS, 2 * LANES)
    flat = (2, CHUNKS, ROWS, LANES)
    any_space = pl.BlockSpec(memory_space=pl.ANY)
    dma = pltpu.SemaphoreType.DMA
    basis, upper = pl.pallas_call(
        functools.partial(kernel, sizes, nodes_total),
        out_shape=(
            jax.ShapeDtypeStruct((VECS, ROWS, LANES), BF16),
            jax.ShapeDtypeStruct((VECS, VECS), F32),
        ),
        in_specs=[any_space] * (4 + TABLES),
        out_specs=(any_space, pl.BlockSpec(memory_space=pltpu.VMEM)),
        scratch_shapes=[pltpu.VMEM(t.shape, t.dtype) for t in tables]
        + [
            pltpu.VMEM((VECS, ROWS, LANES), BF16),
            pltpu.VMEM((PRIOR, ROWS, LANES), BF16),
            pltpu.VMEM((ROWS, LANES), BF16),
            pltpu.VMEM((ROWS, LANES), BF16),
            pltpu.VMEM((VECS, ROWS, LANES), BF16),
            pltpu.VMEM(low, BF16),
            pltpu.VMEM(high, BF16),
            pltpu.VMEM(low, BF16),
            pltpu.VMEM(high, BF16),
            pltpu.VMEM(flat, BF16),
            pltpu.VMEM(low, BF16),
            pltpu.VMEM(high, BF16),
            pltpu.VMEM(low, BF16),
            pltpu.VMEM(high, BF16),
            pltpu.VMEM(flat, BF16),
            pltpu.VMEM(flat, BF16),
            pltpu.VMEM((6, ROWS, LANES), BF16),
            pltpu.VMEM((BLOCK, LANES), F32),
            pltpu.VMEM((ROWS, BLOCK), F32),
            pltpu.VMEM((ROWS, LANES), F32),
            pltpu.VMEM(((VECS + PRIOR) * SIDE, SIDE * LANES), BF16),
            pltpu.VMEM((nz, share, LANES), F32),
            pltpu.VMEM((nz, share, LANES), F32),
            pltpu.VMEM((nx, share, LANES), F32),
            pltpu.VMEM((ny, share, LANES), F32),
            pltpu.VMEM((nz, share, LANES), F32),
            pltpu.VMEM((VECS, ROWS, LANES), BF16),
            dma((3 + TABLES,)),
            dma((CHUNKS,)),
            dma((SIDE // 2,)),
            dma((6,)),
            dma((6,)),
            dma((2, CHUNKS, 6)),
            dma((2, CHUNKS, 6)),
            dma((4, max(sizes))),
            dma((4, max(sizes))),
        ],
        compiler_params=pltpu.CompilerParams(
            collective_id=0, has_side_effects=True, vmem_limit_bytes=56 * 2**20
        ),
    )(
        panel_in.reshape(VECS, ROWS, LANES),
        prior_modes.reshape(PRIOR, ROWS, LANES),
        stiffness.reshape(ROWS, LANES),
        mass_shift.reshape(ROWS, LANES),
        *[jnp.asarray(t) for t in tables],
    )
    return basis.reshape(panel_in.shape), upper


def solution(mesh):
    sizes = tuple(mesh.shape[a] for a in ("gx", "gy", "gz"))
    nodes_total = ROWS * LANES * sizes[0] * sizes[1] * sizes[2]
    placed = (
        P(None, "gx", "gy", "gz"),
        P(None, "gx", "gy", "gz"),
        P("gx", "gy", "gz"),
        P("gx", "gy", "gz"),
    )
    return jax.shard_map(
        functools.partial(on_device, sizes, nodes_total),
        mesh=mesh,
        in_specs=placed,
        out_specs=(P(None, "gx", "gy", "gz"), P()),
        check_vma=False,
    )
```

time: 363 us -> 59.2 us (0.16)
  blocking collectives: 194 us -> 0 us
  Pallas kernels: 0 us -> 55.9 us
  local copies, waits for them, and re-layouts: 45.9 us -> 2.48 us
  waiting for transfers between devices: 39.4 us -> 0 us
  starting transfers between devices: 36.4 us -> 0 us
  other arithmetic: 25.4 us -> 0 us
  matrix products: 20.2 us -> 0 us
    psum x2 -> x0, blocking collectives: 194 us -> none  [the longest x1 98.5 us: on_device(): lax.psum(jnp.dot(flat_p, flat_y.T, preferred_element_type=jnp.float32), (...]
    pallas_call x0 -> x1, Pallas kernels: none -> 55.9 us  [on_device(): pl.pallas_call(functools.partial(kernel, sizes, nodes_total), out_shape=(...]
    ppermute x12 -> x0, waiting for transfers between devices: 39.4 us -> none  [the longest x6 20.7 us: padded(): lax.ppermute(tail, axis, [(i, (i + 1) % count) for i in range(ends)])]
    ppermute x12 -> x0, starting transfers between devices: 36.4 us -> none  [the longest x6 24.1 us: padded(): lax.ppermute(tail, axis, [(i, (i + 1) % count) for i in range(ends)])]
    slice x13 -> x0, local copies, waits for them, and re-layouts: 22.4 us -> none  [the longest x6 12.9 us: padded(): lax.slice_in_dim(cells, cells.shape[dim] - width, cells.shape[dim], axis=...]
    dot_general x15 -> x0, matrix products: 19.9 us -> none  [the longest x2 6.03 us: operate(): jnp.einsum('pa,vpyz->vayz', own_x, (slopes * factor).astype(jnp.bfloat16)...]
    concatenate x5 -> x0, other arithmetic: 17.5 us -> none  [the longest x4 17.5 us: padded(): jnp.concatenate([lax.ppermute(tail, axis, [(i, (i + 1) % count) for i in...]
    ppermute x4 -> x0, local copies, waits for them, and re-layouts: 17.2 us -> none  [the longest x2 9.98 us: padded(): lax.ppermute(tail, axis, [(i, (i + 1) % count) for i in range(ends)])]
  transfers between devices with their start and end apart: 12 -> 0, of which waited for: 9 -> 0; matrix products, arithmetic and copies ran while one was open for 4% -> 0% of each run, Pallas kernels for 0% -> 0%
where the time goes in v1:
time: 59.2 us; the launch traced here: 59.1 us
  Pallas kernels  55.9 us (94%)
  local copies, waits for them, and re-layouts  2.48 us (4%)
  between operations  0.65 us (1%)
    pallas_call x1, Pallas kernels, on_device(): pl.pallas_call(functools.partial(kernel, sizes, nodes_total), out_shape=(...  55.9 us
    unnamed x4, local copies, waits for them, and re-layouts  2.48 us

profile of v1, /device:TPU:1, one launch (start us, length us, event | category | flops | bytes accessed | tf_op | source)
XLA Modules:
  0.0 59.1 jit_solution(6198386256490816873)
XLA Ops:
  0.6 55.9 %shard_map.185 = (bf16[32,64,128]{2,1,0:T(8,128)(2,1)}, f32[32,32]{1,0:T(8,128)}) custom-call(bf16[32,64,128]{2,1,0:T(8,128)(2,1)} %bitcast.6, bf16[64,64,128]{2,1,0:T(8,128)(2,1)} %bitcast.5, bf16[64,128]{1,0:T(8,128)(2,1)} %bitcast.8, bf16[64,128]{1,0:T(8,128)(2,1)} %bitcast.9, bf16[2,256,256]{2,1,0:T(8,128)(2,1)} %constant.28.clone.refs_4_, ...), custom_call_target="tpu_custom_call" | custom-call | tf_op jit(solution)/shard_map/pallas_call | solution.py:573
  56.6 0.0 copy-start
  56.6 1.9 %copy.22 = bf16[32,8,8,128]{3,2,1,0:T(8,128)(2,1)} copy(bf16[32,8,8,128]{3,2,1,0:T(8,128)(2,1)} %bitcast.7) | data formatting | bytes 1048576
  58.4 0.0 copy-done
  58.4 0.6 %copy.23 = f32[32,32]{1,0:T(8,128)} copy(f32[32,32]{1,0:T(8,128)S(1)} %copy-done) | data formatting | bytes 8192
Async XLA Ops:
  56.6 1.9 %copy-start = (f32[32,32]{1,0:T(8,128)S(1)}, f32[32,32]{1,0:T(8,128)}, u32[]{:S(2)}) copy-start(f32[32,32]{1,0:T(8,128)} %get-tuple-element.9) | copy-start | bytes 12292

commit v2 on v1

--- a/solution.py
+++ b/solution.py
@@ -213,14 +213,13 @@
         factor_z,
         shift,
         stack,
-        total_s,
-        scatter_r,
-        sum_x,
-        sum_y,
-        gathered,
+        flux,
+        flux_z,
+        slots_z,
+        slots_x,
+        slots_y,
         result,
         load_sem,
-        field_sem,
         out_sem,
         stiff_send,
         stiff_recv,
@@ -236,25 +235,28 @@
     def along(axis, step):
         return {axes[axis]: lax.rem(me[axis] + step + sizes[axis], sizes[axis])}
 
-    field_loads = []
-    for c in range(CHUNKS):
-        part = pl.ds(c * CHUNK, CHUNK)
-        load = pltpu.make_async_copy(panel.at[part], field.at[part], field_sem.at[c])
-        load.start()
-        field_loads.append(load)
-    loads = []
-    for k, (src, dst) in enumerate(
-        [(stiff, stiff_own), (mass, mass_own), (prior, modes)] + list(zip(tables, held))
-    ):
-        load = pltpu.make_async_copy(src, dst, load_sem.at[k])
-        load.start()
-        loads.append(load)
     barrier = pltpu.get_barrier_semaphore()
     for axis in range(3):
         for step in range(1, sizes[axis]):
             pl.semaphore_signal(
                 barrier, inc=1, device_id=along(axis, step), device_id_type=MESH
             )
+    loads = {}
+
+    def load(name, src, dst):
+        loads[name] = pltpu.make_async_copy(src, dst, load_sem.at[len(loads)])
+        loads[name].start()
+
+    def loaded(*names):
+        for name in names:
+            loads[name].wait()
+
+    load("faces", tables[6], faces)
+    for c in range(CHUNKS):
+        part = pl.ds(c * CHUNK, CHUNK)
+        load(c, panel.at[part], field.at[part])
+    load("ends", tables[7], ends)
+    load("stiff", stiff, stiff_own)
 
     def pack(app, c, source):
         cells = [source[c * CHUNK + j] for j in range(CHUNK)]
@@ -305,15 +307,17 @@
             for k in range(6)
         ]
 
-    for load in loads:
-        load.wait()
-    for load in field_loads:
-        load.wait()
-
-    @pl.loop(0, CHUNKS)
-    def _(c):
+    loaded("faces", "ends")
+    for c in range(CHUNKS):
+        loaded(c)
         pack(0, c, field)
-
+    for k in (0, 2, 3, 5, 11, 12, 13, 1, 4):
+        load("table%d" % k, tables[k], held[k])
+    load("mass", mass, mass_own)
+    load("prior", prior, modes)
+    for k in (8, 9, 10):
+        load("table%d" % k, tables[k], held[k])
+    loaded("stiff")
     pl.semaphore_wait(barrier, nx + ny + nz - 3)
     for copy in stiff_copies():
         copy.start()
@@ -322,6 +326,8 @@
     def _(c):
         for copy in face_copies(0, c):
             copy.start()
+
+    loaded("table0", "table2", "table3", "table5")
 
     first = [me[k] == 0 for k in range(3)]
     last = [me[k] == sizes[k] - 1 for k in range(3)]
@@ -362,7 +368,10 @@
     cut = outside(row, [(LANES, 2 * LANES, first[2]), (2 * LANES, 3 * LANES, last[2])])
     pick_z[...] = jnp.where(cut, 0.0, pick_z[...].astype(F32)).astype(BF16)
 
+    loaded("table11", "table12", "table13", "mass")
     shift[...] = volume[...] * mass_own[...].astype(F32) + filter_center
+
+    loaded("table1", "table4", "table8", "table9", "table10", "prior")
 
     @pl.loop(0, PRIOR // 2)
     def _(p):
@@ -392,14 +401,21 @@
         joined = jnp.where(
             slot < 3, low_z_r[app, c].astype(F32), high_z_r[app, c].astype(F32)
         )
+        cells = [source[c * CHUNK + j] for j in range(CHUNK)]
+        lines = []
+        for j in range(CHUNK):
+            rolled = pltpu.roll(joined, LANES - SLOT * j, 1) if j else joined
+            lines.append(jnp.concatenate([cells[j], rolled.astype(BF16)], axis=1))
+        factor_rows = jnp.concatenate([factor_z[...]] * CHUNK, axis=0)
+        flux_z[...] = (
+            dot(jnp.concatenate(lines, axis=0), grad_z[...]) * factor_rows
+        ).astype(BF16)
         factor_two = jnp.concatenate([factor[...], factor[...]], axis=1)
-        factor_rows = jnp.concatenate([factor_z[...], factor_z[...]], axis=0)
         for p in range(PAIRS):
             q, parity = p // 2, p % 2
-            cells = [source[c * CHUNK + 2 * p + h] for h in range(2)]
             rows = jnp.concatenate(
                 [
-                    jnp.concatenate(cells, axis=1),
+                    jnp.concatenate(cells[2 * p : 2 * p + 2], axis=1),
                     high_x_r[app, c, 16 * p : 16 * p + 16],
                     high_y_r[app, c, 16 * p : 16 * p + 16],
                     low_x_r[app, c, 48 * q : 48 * q + 48],
@@ -408,21 +424,14 @@
                 ],
                 axis=0,
             )
-            flux = (dot(grad[parity], rows) * factor_two).astype(BF16)
-            image = dot(back[...], flux)
-            lines = []
-            for h in range(2):
-                j = 2 * p + h
-                rolled = pltpu.roll(joined, LANES - SLOT * j, 1) if j else joined
-                lines.append(jnp.concatenate([cells[h], rolled.astype(BF16)], axis=1))
-            flux_z = (dot(jnp.concatenate(lines, axis=0), grad_z[...]) * factor_rows).astype(
-                BF16
-            )
-            image_z = dot(flux_z, back_z[...])
+            flux[p] = (dot(grad[parity], rows) * factor_two).astype(BF16)
+        image_z = dot(flux_z[...], back_z[...])
+        for p in range(PAIRS):
+            image = dot(back[...], flux[p])
             moved = [
                 image[:, h * LANES : (h + 1) * LANES]
-                + image_z[h * ROWS : (h + 1) * ROWS]
-                - shift[...] * cells[h].astype(F32)
+                + image_z[(2 * p + h) * ROWS : (2 * p + h + 1) * ROWS]
+                - shift[...] * cells[2 * p + h].astype(F32)
                 for h in range(2)
             ]
             finish(c, p, moved)
@@ -465,45 +474,44 @@
     folded = sum(dot(fold[...], t) for t in split3(jnp.where(same, cross, 0.0)))
     sums = sum(dot(t, gather[...]) for t in split3(folded))
 
-    share = VECS // nz
-
-    def sum_copies(stage, axis, source, target):
-        copies = []
-        for step in range(1, sizes[axis]):
-            to = lax.rem(me[axis] + step, sizes[axis])
-            copies.append(
-                pltpu.make_async_remote_copy(
-                    src_ref=source(to),
-                    dst_ref=target(step),
-                    send_sem=sum_send.at[stage, step],
-                    recv_sem=sum_recv.at[stage, step],
-                    device_id={axes[axis]: to},
-                    device_id_type=MESH,
-                )
+    lane = side((8, LANES), 1)
+    used = VECS + PRIOR
+    tail = sums[24:]
+    mine = jnp.concatenate(
+        [
+            jnp.where(lane < used, sums[8 * r : 8 * r + 8], pltpu.roll(tail, used - 32 * r, 1))
+            for r in range(3)
+        ],
+        axis=0,
+    )
+    sent = []
+    for stage, (axis, slots) in enumerate(((2, slots_z), (0, slots_x), (1, slots_y))):
+        slots[me[axis]] = mine
+        here = slots.at[me[axis]]
+        copies = [
+            pltpu.make_async_remote_copy(
+                src_ref=here,
+                dst_ref=here,
+                send_sem=sum_send.at[stage, step],
+                recv_sem=sum_recv.at[stage, step],
+                device_id=along(axis, step),
+                device_id_type=MESH,
             )
+            for step in range(1, sizes[axis])
+        ]
         for copy in copies:
             copy.start()
         for copy in copies:
             copy.wait_recv()
-        return copies
-
-    for k in range(nz):
-        total_s[k] = sums[k * share : (k + 1) * share]
-    sent = sum_copies(0, 2, lambda to: total_s.at[to], lambda step: scatter_r.at[step])
-    mine = total_s[me[2]]
-    for step in range(1, nz):
-        mine = mine + scatter_r[step]
-    for stage, axis, slots in ((1, 0, sum_x), (2, 1, sum_y)):
-        slots[me[axis]] = mine
-        here = slots.at[me[axis]]
-        sent += sum_copies(stage, axis, lambda to: here, lambda step: here)
+        sent += copies
         mine = slots[0]
         for k in range(1, sizes[axis]):
             mine = mine + slots[k]
-    gathered[me[2]] = mine
-    here = gathered.at[me[2]]
-    sent += sum_copies(3, 2, lambda to: here, lambda step: here)
-    sums = jnp.concatenate([gathered[k] for k in range(nz)], axis=0) * (1.0 / nodes_total)
+    tail = jnp.zeros((8, LANES), F32)
+    for r in range(3):
+        part = pltpu.roll(mine[8 * r : 8 * r + 8], LANES - used + 32 * r, 1)
+        tail = jnp.where((lane >= 32 * r) & (lane < 32 * r + 32), part, tail)
+    sums = jnp.concatenate([mine, tail], axis=0) * (1.0 / nodes_total)
 
     lane = side((VECS, LANES), 1)
     line = side((VECS, LANES), 0)
@@ -563,7 +571,6 @@
 
 def on_device(sizes, nodes_total, panel_in, prior_modes, stiffness, mass_shift):
     nx, ny, nz = sizes
-    share = VECS // nz
     tables = make_tables()
     low = (2, CHUNKS, 24 * PAIRS, 2 * LANES)
     high = (2, CHUNKS, 16 * PAIRS, 2 * LANES)
@@ -601,21 +608,20 @@
             pltpu.VMEM((ROWS, BLOCK), F32),
             pltpu.VMEM((ROWS, LANES), F32),
             pltpu.VMEM(((VECS + PRIOR) * SIDE, SIDE * LANES), BF16),
-            pltpu.VMEM((nz, share, LANES), F32),
-            pltpu.VMEM((nz, share, LANES), F32),
-            pltpu.VMEM((nx, share, LANES), F32),
-            pltpu.VMEM((ny, share, LANES), F32),
-            pltpu.VMEM((nz, share, LANES), F32),
+            pltpu.VMEM((PAIRS, BLOCK, 2 * LANES), BF16),
+            pltpu.VMEM((CHUNK * ROWS, BLOCK), BF16),
+            pltpu.VMEM((nz, 24, LANES), F32),
+            pltpu.VMEM((nx, 24, LANES), F32),
+            pltpu.VMEM((ny, 24, LANES), F32),
             pltpu.VMEM((VECS, ROWS, LANES), BF16),
-            dma((3 + TABLES,)),
-            dma((CHUNKS,)),
+            dma((3 + CHUNKS + TABLES,)),
             dma((SIDE // 2,)),
             dma((6,)),
             dma((6,)),
             dma((2, CHUNKS, 6)),
             dma((2, CHUNKS, 6)),
-            dma((4, max(sizes))),
-            dma((4, max(sizes))),
+            dma((3, max(sizes))),
+            dma((3, max(sizes))),
         ],
         compiler_params=pltpu.CompilerParams(
             collective_id=0, has_side_effects=True, vmem_limit_bytes=56 * 2**20

time: 59.2 us -> 52 us (0.88)
  Pallas kernels: 55.9 us -> 48.7 us
    pallas_call x1, Pallas kernels: 55.9 us -> 48.7 us  [on_device(): pl.pallas_call(functools.partial(kernel, sizes, nodes_total), out_shape=(...]
where the time goes in v2:
time: 52 us; the launch traced here: 51.8 us
  Pallas kernels  48.7 us (94%)
  local copies, waits for them, and re-layouts  2.48 us (5%)
  between operations  0.65 us (1%)
    pallas_call x1, Pallas kernels, on_device(): pl.pallas_call(functools.partial(kernel, sizes, nodes_total), out_shape=(...  48.7 us
    unnamed x4, local copies, waits for them, and re-layouts  2.48 us

profile of v2, /device:TPU:1, one launch (start us, length us, event | category | flops | bytes accessed | tf_op | source)
XLA Modules:
  0.0 51.8 jit_solution(410090465483531794)
XLA Ops:
  0.6 48.7 %shard_map.185 = (bf16[32,64,128]{2,1,0:T(8,128)(2,1)}, f32[32,32]{1,0:T(8,128)}) custom-call(bf16[32,64,128]{2,1,0:T(8,128)(2,1)} %bitcast.6, bf16[64,64,128]{2,1,0:T(8,128)(2,1)} %bitcast.5, bf16[64,128]{1,0:T(8,128)(2,1)} %bitcast.8, bf16[64,128]{1,0:T(8,128)(2,1)} %bitcast.9, bf16[2,256,256]{2,1,0:T(8,128)(2,1)} %constant.28.clone.refs_4_, ...), custom_call_target="tpu_custom_call" | custom-call | tf_op jit(solution)/shard_map/pallas_call | solution.py:580
  49.3 0.0 copy-start
  49.4 1.9 %copy.22 = bf16[32,8,8,128]{3,2,1,0:T(8,128)(2,1)} copy(bf16[32,8,8,128]{3,2,1,0:T(8,128)(2,1)} %bitcast.7) | data formatting | bytes 1048576
  51.2 0.0 copy-done
  51.2 0.6 %copy.23 = f32[32,32]{1,0:T(8,128)} copy(f32[32,32]{1,0:T(8,128)S(1)} %copy-done) | data formatting | bytes 8192
Async XLA Ops:
  49.3 1.9 %copy-start = (f32[32,32]{1,0:T(8,128)S(1)}, f32[32,32]{1,0:T(8,128)}, u32[]{:S(2)}) copy-start(f32[32,32]{1,0:T(8,128)} %get-tuple-element.9) | copy-start | bytes 12292

commit v3 on v2

--- a/solution.py
+++ b/solution.py
@@ -135,23 +135,10 @@
             for j in range(3):
                 faces[32 + 24 * half + j * SIDE + t, 64 * half + (5 + j) * SIDE + t] = 1
                 faces[80 + 24 * half + j * SIDE + t, 64 * half + t * SIDE + 5 + j] = 1
-    ends = np.zeros((CHUNK * LANES, LANES))
-    for j in range(CHUNK):
-        for i in range(5):
-            ends[j * LANES + (LANES - 3 + i) % LANES, j * SLOT + i] = 1
     volume = np.zeros((ROWS, LANES))
     for t in range(ROWS):
         volume[t] = node_w[t // SIDE] * node_w[t % SIDE] * node_z
-    fold = np.zeros((VECS, VECS * SIDE))
-    for v in range(VECS):
-        fold[v, v * SIDE : (v + 1) * SIDE] = 1
-    spread = np.zeros((2 * VECS * SIDE, 2 * VECS))
-    for v in range(2 * VECS):
-        spread[v * SIDE : (v + 1) * SIDE, v] = 1
-    gather = np.zeros(((VECS + PRIOR) * SIDE, LANES))
-    for u in range(VECS + PRIOR):
-        gather[u * SIDE : (u + 1) * SIDE, u] = 1
-    halves = [grad, back, pick, grad_z, back_z, pick_z, faces, ends, fold, spread, gather]
+    halves = [grad, back, pick, grad_z, back_z, pick_z, faces]
     singles = [scale, scale_z, volume]
     return [t.astype(np.float32).astype(ml_dtypes.bfloat16) for t in halves] + [
         t.astype(np.float32) for t in singles
@@ -168,29 +155,20 @@
     )
 
 
-def split3(a):
-    first = a.astype(BF16)
-    rest = a - first.astype(F32)
-    second = rest.astype(BF16)
-    third = (rest - second.astype(F32)).astype(BF16)
-    return first, second, third
-
-
 def side(shape, dim):
     return lax.broadcasted_iota(jnp.int32, shape, dim)
 
 
-TABLES = 14
+TABLES = 10
 
 
 def kernel(sizes, nodes_total, *refs):
     panel, prior, stiff, mass = refs[:4]
     tables = refs[4 : 4 + TABLES]
-    out, upper = refs[4 + TABLES : 6 + TABLES]
+    rows_out, sums_out = refs[4 + TABLES : 6 + TABLES]
     scratch = refs[6 + TABLES :]
     held = scratch[:TABLES]
-    grad, back, pick, grad_z, back_z, pick_z, faces, ends, fold, spread, gather = held[:11]
-    scale, scale_z, volume = held[11:]
+    grad, back, pick, grad_z, back_z, pick_z, faces, scale, scale_z, volume = held
     (
         field,
         modes,
@@ -212,15 +190,15 @@
         factor,
         factor_z,
         shift,
-        stack,
+        whole,
+        image_rows,
         flux,
         flux_z,
         slots_z,
         slots_x,
         slots_y,
-        result,
         load_sem,
-        out_sem,
+        rows_sem,
         stiff_send,
         stiff_recv,
         face_send,
@@ -252,11 +230,10 @@
             loads[name].wait()
 
     load("faces", tables[6], faces)
+    load("stiff", stiff, stiff_own)
     for c in range(CHUNKS):
         part = pl.ds(c * CHUNK, CHUNK)
         load(c, panel.at[part], field.at[part])
-    load("ends", tables[7], ends)
-    load("stiff", stiff, stiff_own)
 
     def pack(app, c, source):
         cells = [source[c * CHUNK + j] for j in range(CHUNK)]
@@ -271,7 +248,12 @@
             high_y_s[app, c, 32 * q : 32 * q + 32] = picked[:32]
             low_x_s[app, c, 48 * q : 48 * q + 48] = picked[32:80]
             low_y_s[app, c, 48 * q : 48 * q + 48] = picked[80:]
-        ends_s[app, c] = dot(jnp.concatenate(cells, axis=1), ends[...]).astype(BF16)
+        lane = side((ROWS, LANES), 1)
+        edges = jnp.zeros((ROWS, LANES), F32)
+        for j in range(CHUNK):
+            here = (lane >= SLOT * j) & (lane < SLOT * j + 5)
+            edges = jnp.where(here, pltpu.roll(cells[j].astype(F32), SLOT * j + 3, 1), edges)
+        ends_s[app, c] = edges.astype(BF16)
 
     def face_copies(app, c):
         plan = [
@@ -307,23 +289,19 @@
             for k in range(6)
         ]
 
-    loaded("faces", "ends")
+    loaded("faces", "stiff")
     for c in range(CHUNKS):
         loaded(c)
+        if c == 0:
+            for k in (0, 2, 3, 5, 7, 8, 9, 1, 4):
+                load("table%d" % k, tables[k], held[k])
+            load("mass", mass, mass_own)
+            load("prior", prior, modes)
         pack(0, c, field)
-    for k in (0, 2, 3, 5, 11, 12, 13, 1, 4):
-        load("table%d" % k, tables[k], held[k])
-    load("mass", mass, mass_own)
-    load("prior", prior, modes)
-    for k in (8, 9, 10):
-        load("table%d" % k, tables[k], held[k])
-    loaded("stiff")
-    pl.semaphore_wait(barrier, nx + ny + nz - 3)
-    for copy in stiff_copies():
-        copy.start()
-
-    @pl.loop(0, CHUNKS)
-    def _(c):
+        if c == 0:
+            pl.semaphore_wait(barrier, nx + ny + nz - 3)
+            for copy in stiff_copies():
+                copy.start()
         for copy in face_copies(0, c):
             copy.start()
 
@@ -368,21 +346,30 @@
     cut = outside(row, [(LANES, 2 * LANES, first[2]), (2 * LANES, 3 * LANES, last[2])])
     pick_z[...] = jnp.where(cut, 0.0, pick_z[...].astype(F32)).astype(BF16)
 
-    loaded("table11", "table12", "table13", "mass")
+    loaded("table7", "table8", "table9", "mass")
     shift[...] = volume[...] * mass_own[...].astype(F32) + filter_center
 
-    loaded("table1", "table4", "table8", "table9", "table10", "prior")
-
-    @pl.loop(0, PRIOR // 2)
-    def _(p):
-        one = modes[2 * p].astype(F32)
-        two = modes[2 * p + 1].astype(F32)
-        at = pl.ds(pl.multiple_of(VECS * SIDE + 16 * p, 16), 16)
+    loaded("table1", "table4", "prior")
+
+    def place(at, cells):
         for x in range(SIDE):
             rows = slice(x * SIDE, (x + 1) * SIDE)
-            stack[at, x * LANES : (x + 1) * LANES] = jnp.concatenate(
-                [one[rows], two[rows]], axis=0
-            ).astype(BF16)
+            block = jnp.stack([cell[rows] for cell in cells], axis=0)
+            block = jnp.swapaxes(block, 0, 1).astype(BF16)
+            for y in range(SIDE):
+                first_lane = (x * SIDE + y) * LANES
+                whole[at, first_lane : first_lane + LANES] = block[y]
+
+    @pl.loop(0, PRIOR // 16)
+    def _(g):
+        at = pl.ds(pl.multiple_of(VECS + 16 * g, 16), 16)
+        place(at, [modes[16 * g + j].astype(F32) for j in range(16)])
+
+    rows_writes = [
+        pltpu.make_async_copy(whole.at[part], rows_out.at[part], rows_sem.at[k])
+        for k, part in enumerate([pl.ds(VECS, PRIOR), pl.ds(0, VECS)])
+    ]
+    rows_writes[0].start()
 
     for copy in stiff_copies():
         copy.wait_recv()
@@ -441,16 +428,10 @@
             once[c * CHUNK + 2 * p + h] = (moved[h] * (1.0 / filter_half)).astype(BF16)
 
     def finish_two(c, p, moved):
-        done = [
-            moved[h] * (2.0 / filter_half) - field[c * CHUNK + 2 * p + h].astype(F32)
-            for h in range(2)
-        ]
-        at = pl.ds(pl.multiple_of(c * (CHUNK * SIDE) + 16 * p, 16), 16)
-        for x in range(SIDE):
-            rows = slice(x * SIDE, (x + 1) * SIDE)
-            stack[at, x * LANES : (x + 1) * LANES] = jnp.concatenate(
-                [done[0][rows], done[1][rows]], axis=0
-            ).astype(BF16)
+        for h in range(2):
+            j = c * CHUNK + 2 * p + h
+            done = moved[h] * (2.0 / filter_half) - field[j].astype(F32)
+            image_rows[lax.rem(j, 16)] = done
 
     @pl.loop(0, CHUNKS)
     def _(c):
@@ -461,18 +442,19 @@
         for copy in face_copies(1, c):
             copy.start()
 
-    @pl.loop(0, CHUNKS)
-    def _(c):
-        for copy in face_copies(1, c):
-            copy.wait_recv()
-        operate(1, c, once, finish_two)
-
-    wide = VECS * SIDE
-    tall = (VECS + PRIOR) * SIDE
-    cross = dot_nt(stack[:wide], stack[...])
-    same = lax.rem(side((wide, tall), 0), SIDE) == lax.rem(side((wide, tall), 1), SIDE)
-    folded = sum(dot(fold[...], t) for t in split3(jnp.where(same, cross, 0.0)))
-    sums = sum(dot(t, gather[...]) for t in split3(folded))
+    @pl.loop(0, VECS // 16)
+    def _(g):
+        for k in range(16 // CHUNK):
+            c = g * (16 // CHUNK) + k
+            for copy in face_copies(1, c):
+                copy.wait_recv()
+            operate(1, c, once, finish_two)
+        at = pl.ds(pl.multiple_of(16 * g, 16), 16)
+        place(at, [image_rows[j] for j in range(16)])
+
+    rows_writes[1].start()
+    sums = dot_nt(whole[:VECS], whole[...])
+    sums = jnp.concatenate([sums, jnp.zeros((VECS, LANES - VECS - PRIOR), F32)], axis=1)
 
     lane = side((8, LANES), 1)
     used = VECS + PRIOR
@@ -511,50 +493,7 @@
     for r in range(3):
         part = pltpu.roll(mine[8 * r : 8 * r + 8], LANES - used + 32 * r, 1)
         tail = jnp.where((lane >= 32 * r) & (lane < 32 * r + 32), part, tail)
-    sums = jnp.concatenate([mine, tail], axis=0) * (1.0 / nodes_total)
-
-    lane = side((VECS, LANES), 1)
-    line = side((VECS, LANES), 0)
-    proj = jnp.where((lane >= VECS) & (lane < VECS + PRIOR), sums, 0.0)
-    coeffs = proj.astype(BF16).astype(F32)
-    rest = proj - coeffs
-    exact = lax.Precision.HIGHEST
-    gram = sums[:, :VECS] - dot_nt(proj, proj, exact) + dot_nt(rest, rest, exact)
-    solve = jnp.where(lane == line, 1.0, 0.0) - coeffs
-    below = side((VECS, 1), 0)
-    for k in range(VECS):
-        ratio = jnp.where(below > k, gram[:, k : k + 1] / gram[k : k + 1, k : k + 1], 0.0)
-        solve = solve - ratio * solve[k : k + 1]
-        gram = gram - ratio * gram[k : k + 1]
-    left = side((VECS, VECS), 0)
-    right = side((VECS, VECS), 1)
-    pivots = jnp.sum(jnp.where(left == right, gram, 0.0), axis=1, keepdims=True)
-    inverse = 1.0 / jnp.sqrt(pivots)
-    upper[...] = jnp.where(right >= left, gram * inverse, 0.0)
-    solve = solve * inverse
-
-    high = solve.astype(BF16)
-    low = (solve - high.astype(F32)).astype(BF16)
-    widened = dot_nt(jnp.concatenate([high, low], axis=0), gather[...]).astype(BF16)
-    widened = dot(spread[...], widened)
-    shape = (2 * wide, tall)
-    same = lax.rem(side(shape, 0), SIDE) == lax.rem(side(shape, 1), SIDE)
-    widened = jnp.where(same, widened, 0.0).astype(BF16)
-    writes = []
-    for x in range(0, SIDE, 2):
-        block = dot(widened, stack[:, x * LANES : (x + 2) * LANES])
-        block = block[:wide] + block[wide:]
-        for v in range(VECS):
-            rows = block[v * SIDE : (v + 1) * SIDE]
-            result[v, x * SIDE : (x + 2) * SIDE] = jnp.concatenate(
-                [rows[:, :LANES], rows[:, LANES:]], axis=0
-            ).astype(BF16)
-        part = pl.ds(x * SIDE, 2 * SIDE)
-        write = pltpu.make_async_copy(
-            result.at[:, part], out.at[:, part], out_sem.at[x // 2]
-        )
-        write.start()
-        writes.append(write)
+    sums_out[...] = jnp.concatenate([mine, tail], axis=0)
 
     for copy in sent + stiff_copies():
         copy.wait_send()
@@ -565,6 +504,91 @@
             for copy in face_copies(app, c):
                 copy.wait_send()
 
+    for write in rows_writes:
+        write.wait()
+
+
+def finish_kernel(nodes_total, rows_in, sums_in, out, upper, whole, result, rows_sem, out_sem):
+    width = 2 * SIDE * LANES
+    parts = SIDE // 2
+    loads = []
+    for k in range(parts):
+        part = pl.ds(k * width, width)
+        load = pltpu.make_async_copy(rows_in.at[:, part], whole.at[:, part], rows_sem.at[k])
+        load.start()
+        loads.append(load)
+
+    lane = side((VECS, LANES), 1)
+    line = side((VECS, LANES), 0)
+    sums = sums_in[...] * (1.0 / nodes_total)
+    proj = jnp.where((lane >= VECS) & (lane < VECS + PRIOR), sums, 0.0)
+    coeffs = proj.astype(BF16)
+    rest = proj - coeffs.astype(F32)
+    rest_high = rest.astype(BF16)
+    rest_low = (rest - rest_high.astype(F32)).astype(BF16)
+    left = jnp.concatenate([coeffs, coeffs, coeffs, rest_high, rest_low], axis=1)
+    right = jnp.concatenate([coeffs, rest_high, rest_low, coeffs, coeffs], axis=1)
+    right = jnp.concatenate([right, jnp.zeros((LANES - VECS, 5 * LANES), BF16)], axis=0)
+    state = jnp.where(lane < VECS, sums - dot_nt(left, right), 0.0)
+    state = jnp.where(lane == line + VECS, 1.0, state)
+    state = state - pltpu.roll(coeffs.astype(F32), VECS, 1)
+
+    step = 8
+
+    def rows_of(value):
+        return jnp.concatenate([value] * (VECS // 8), axis=0)
+
+    for first in range(0, VECS, step):
+        cols = [
+            jnp.broadcast_to(state[:, first + j : first + j + 1], (VECS, LANES))
+            for j in range(step)
+        ]
+        lines = [
+            jnp.broadcast_to(state[first + j : first + j + 1], (8, LANES)) for j in range(step)
+        ]
+        pivots = [
+            [jnp.broadcast_to(cols[j][first + i : first + i + 1], (8, LANES)) for j in range(step)]
+            for i in range(step)
+        ]
+        ratios = []
+        for j in range(step):
+            inverse = 1.0 / pivots[j][j]
+            ratio = jnp.where(line > first + j, cols[j] * rows_of(inverse), 0.0)
+            ratios.append(ratio)
+            for i in range(j + 1, step):
+                times = pivots[i][j] * inverse
+                for t in range(j + 1, step):
+                    pivots[i][t] = pivots[i][t] - times * pivots[j][t]
+                lines[i] = lines[i] - times * lines[j]
+                cols[i] = cols[i] - ratio * rows_of(pivots[j][i])
+        for j in range(step):
+            state = state - ratios[j] * rows_of(lines[j])
+    diagonal = jnp.sum(jnp.where(lane == line, state, 0.0), axis=1, keepdims=True)
+    state = state * (1.0 / jnp.sqrt(diagonal))
+    upper[...] = jnp.where(lane >= line, state, 0.0)[:, :VECS]
+
+    solve = pltpu.roll(state, LANES - VECS, 1)[:, : VECS + PRIOR]
+    high = solve.astype(BF16)
+    low = (solve - high.astype(F32)).astype(BF16)
+    solve = jnp.concatenate([high, low], axis=0)
+    writes = []
+    for k in range(parts):
+        loads[k].wait()
+        blocks = []
+        for x in (2 * k, 2 * k + 1):
+            block = dot(solve, whole[:, x * SIDE * LANES : (x + 1) * SIDE * LANES])
+            block = block[:VECS] + block[VECS:]
+            block = jnp.stack(
+                [block[:, y * LANES : (y + 1) * LANES] for y in range(SIDE)], axis=0
+            )
+            blocks.append(jnp.swapaxes(block, 0, 1))
+        at = slice(2 * k * SIDE, 2 * (k + 1) * SIDE)
+        for v in range(VECS):
+            result[v, at] = jnp.concatenate([blocks[0][v], blocks[1][v]], axis=0).astype(BF16)
+        part = pl.ds(2 * k * SIDE, 2 * SIDE)
+        write = pltpu.make_async_copy(result.at[:, part], out.at[:, part], out_sem.at[k])
+        write.start()
+        writes.append(write)
     for write in writes:
         write.wait()
 
@@ -577,11 +601,11 @@
     flat = (2, CHUNKS, ROWS, LANES)
     any_space = pl.BlockSpec(memory_space=pl.ANY)
     dma = pltpu.SemaphoreType.DMA
-    basis, upper = pl.pallas_call(
+    rows, sums = pl.pallas_call(
         functools.partial(kernel, sizes, nodes_total),
         out_shape=(
-            jax.ShapeDtypeStruct((VECS, ROWS, LANES), BF16),
-            jax.ShapeDtypeStruct((VECS, VECS), F32),
+            jax.ShapeDtypeStruct((VECS + PRIOR, ROWS * LANES), BF16),
+            jax.ShapeDtypeStruct((VECS, LANES), F32),
         ),
         in_specs=[any_space] * (4 + TABLES),
         out_specs=(any_space, pl.BlockSpec(memory_space=pltpu.VMEM)),
@@ -607,15 +631,15 @@
             pltpu.VMEM((BLOCK, LANES), F32),
             pltpu.VMEM((ROWS, BLOCK), F32),
             pltpu.VMEM((ROWS, LANES), F32),
-            pltpu.VMEM(((VECS + PRIOR) * SIDE, SIDE * LANES), BF16),
+            pltpu.VMEM((VECS + PRIOR, ROWS * LANES), BF16),
+            pltpu.VMEM((16, ROWS, LANES), F32),
             pltpu.VMEM((PAIRS, BLOCK, 2 * LANES), BF16),
             pltpu.VMEM((CHUNK * ROWS, BLOCK), BF16),
             pltpu.VMEM((nz, 24, LANES), F32),
             pltpu.VMEM((nx, 24, LANES), F32),
             pltpu.VMEM((ny, 24, LANES), F32),
-            pltpu.VMEM((VECS, ROWS, LANES), BF16),
             dma((3 + CHUNKS + TABLES,)),
-            dma((SIDE // 2,)),
+            dma((2,)),
             dma((6,)),
             dma((6,)),
             dma((2, CHUNKS, 6)),
@@ -633,6 +657,22 @@
         mass_shift.reshape(ROWS, LANES),
         *[jnp.asarray(t) for t in tables],
     )
+    basis, upper = pl.pallas_call(
+        functools.partial(finish_kernel, nodes_total),
+        out_shape=(
+            jax.ShapeDtypeStruct((VECS, ROWS, LANES), BF16),
+            jax.ShapeDtypeStruct((VECS, VECS), F32),
+        ),
+        in_specs=[any_space, pl.BlockSpec(memory_space=pltpu.VMEM)],
+        out_specs=(any_space, pl.BlockSpec(memory_space=pltpu.VMEM)),
+        scratch_shapes=[
+            pltpu.VMEM((VECS + PRIOR, ROWS * LANES), BF16),
+            pltpu.VMEM((VECS, ROWS, LANES), BF16),
+            dma((SIDE // 2,)),
+            dma((SIDE // 2,)),
+        ],
+        compiler_params=pltpu.CompilerParams(vmem_limit_bytes=56 * 2**20),
+    )(rows, sums)
     return basis.reshape(panel_in.shape), upper
 
 

time: 52 us -> 49.2 us (0.946)
  local copies, waits for them, and re-layouts: 2.48 us -> 0 us
    pallas_call x1, Pallas kernels: 48.7 us -> 43.3 us  [on_device(): pl.pallas_call(functools.partial(kernel, sizes, nodes_total), out_shape=(...]
    pallas_call x0 -> x1, Pallas kernels: none -> 4.97 us  [on_device(): pl.pallas_call(functools.partial(finish_kernel, nodes_total), out_shape=(...]
    unnamed x4 -> x0, local copies, waits for them, and re-layouts: 2.48 us -> none
where the time goes in v3:
time: 49.2 us; the launch traced here: 48.9 us
  Pallas kernels  48.3 us (98%)
  between operations  0.64 us (1%)
    pallas_call x1, Pallas kernels, on_device(): pl.pallas_call(functools.partial(kernel, sizes, nodes_total), out_shape=(...  43.3 us
    pallas_call x1, Pallas kernels, on_device(): pl.pallas_call(functools.partial(finish_kernel, nodes_total), out_shape=(...  4.97 us

profile of v3, /device:TPU:1, one launch (start us, length us, event | category | flops | bytes accessed | tf_op | source)
XLA Modules:
  0.0 48.9 jit_solution(18241885762262806376)
XLA Ops:
  0.6 43.3 %shard_map.149 = (bf16[96,8192]{1,0:T(8,128)(2,1)}, f32[32,128]{1,0:T(8,128)}) custom-call(bf16[32,64,128]{2,1,0:T(8,128)(2,1)} %bitcast.6, bf16[64,64,128]{2,1,0:T(8,128)(2,1)} %bitcast.5, bf16[64,128]{1,0:T(8,128)(2,1)} %bitcast.7, bf16[64,128]{1,0:T(8,128)(2,1)} %bitcast.8, bf16[2,256,256]{2,1,0:T(8,128)(2,1)} %constant.20.clone.refs_4_, ...), custom_call_target="tpu_custom_call" | custom-call | tf_op jit(solution)/shard_map/pallas_call | solution.py:604
  44.0 5.0 %shard_map.150 = (bf16[32,64,128]{2,1,0:T(8,128)(2,1)}, f32[32,32]{1,0:T(8,128)}) custom-call(bf16[96,8192]{1,0:T(8,128)(2,1)} %get-tuple-element.6.rows_in, f32[32,128]{1,0:T(8,128)} %get-tuple-element.7.sums_in), custom_call_target="tpu_custom_call" | custom-call | tf_op jit(solution)/shard_map/pallas_call | solution.py:660

commit v4 on v3

--- a/solution.py
+++ b/solution.py
@@ -50,6 +50,7 @@
 
 HIGH_X, HIGH_Y, LOW_X, LOW_Y = 64, 80, 96, 144
 BLOCK = 256
+LOW_X_R, LOW_Y_R, HIGH_X_R, HIGH_Y_R = 0, 96, 192, 256
 
 
 def field_row(x, y, parity):
@@ -165,7 +166,7 @@
 def kernel(sizes, nodes_total, *refs):
     panel, prior, stiff, mass = refs[:4]
     tables = refs[4 : 4 + TABLES]
-    rows_out, sums_out = refs[4 + TABLES : 6 + TABLES]
+    whole, sums_out = refs[4 + TABLES : 6 + TABLES]
     scratch = refs[6 + TABLES :]
     held = scratch[:TABLES]
     grad, back, pick, grad_z, back_z, pick_z, faces, scale, scale_z, volume = held
@@ -176,21 +177,16 @@
         mass_own,
         once,
         low_x_s,
+        low_y_s,
         high_x_s,
-        low_y_s,
         high_y_s,
         ends_s,
-        low_x_r,
-        high_x_r,
-        low_y_r,
-        high_y_r,
-        low_z_r,
-        high_z_r,
+        faces_r,
+        ends_r,
         stiff_r,
         factor,
         factor_z,
         shift,
-        whole,
         image_rows,
         flux,
         flux_z,
@@ -198,13 +194,12 @@
         slots_x,
         slots_y,
         load_sem,
-        rows_sem,
-        stiff_send,
-        stiff_recv,
-        face_send,
-        face_recv,
+        send_sem,
+        recv_sem,
+        stiff_sem,
         sum_send,
         sum_recv,
+        token,
     ) = scratch[TABLES:]
     nx, ny, nz = sizes
     axes = ("gx", "gy", "gz")
@@ -214,11 +209,15 @@
         return {axes[axis]: lax.rem(me[axis] + step + sizes[axis], sizes[axis])}
 
     barrier = pltpu.get_barrier_semaphore()
-    for axis in range(3):
-        for step in range(1, sizes[axis]):
-            pl.semaphore_signal(
-                barrier, inc=1, device_id=along(axis, step), device_id_type=MESH
-            )
+
+    def greet(semaphore):
+        for axis in range(3):
+            for step in (1, -1):
+                pl.semaphore_signal(
+                    semaphore, inc=1, device_id=along(axis, step), device_id_type=MESH
+                )
+
+    greet(barrier)
     loads = {}
 
     def load(name, src, dst):
@@ -257,32 +256,45 @@
 
     def face_copies(app, c):
         plan = [
-            (low_x_s, low_x_r, 0, 1),
-            (high_x_s, high_x_r, 0, -1),
-            (low_y_s, low_y_r, 1, 1),
-            (high_y_s, high_y_r, 1, -1),
-            (ends_s, low_z_r, 2, 1),
-            (ends_s, high_z_r, 2, -1),
+            (low_x_s, LOW_X_R, 0, 1),
+            (high_x_s, HIGH_X_R, 0, -1),
+            (low_y_s, LOW_Y_R, 1, 1),
+            (high_y_s, HIGH_Y_R, 1, -1),
+            (ends_s, 0, 2, 1),
+            (ends_s, 1, 2, -1),
         ]
-        return [
-            pltpu.make_async_remote_copy(
-                src_ref=src.at[app, c],
-                dst_ref=dst.at[app, c],
-                send_sem=face_send.at[app, c, k],
-                recv_sem=face_recv.at[app, c, k],
-                device_id=along(axis, step),
-                device_id_type=MESH,
+        copies = []
+        for k, (src, at, axis, step) in enumerate(plan):
+            if axis == 2:
+                target = ends_r.at[app, c, at]
+            else:
+                target = faces_r.at[app, c, pl.ds(at, src.shape[2])]
+            copies.append(
+                pltpu.make_async_remote_copy(
+                    src_ref=src.at[app, c],
+                    dst_ref=target,
+                    send_sem=send_sem.at[k],
+                    recv_sem=recv_sem.at[app, c, axis // 2],
+                    device_id=along(axis, step),
+                    device_id_type=MESH,
+                )
             )
-            for k, (src, dst, axis, step) in enumerate(plan)
-        ]
+        return copies
+
+    def arrived(buffer, semaphore):
+        pltpu.make_async_copy(buffer, buffer, semaphore).wait()
+
+    def faces_arrived(app, c):
+        arrived(faces_r.at[app, c], recv_sem.at[app, c, 0])
+        arrived(ends_r.at[app, c], recv_sem.at[app, c, 1])
 
     def stiff_copies():
         return [
             pltpu.make_async_remote_copy(
                 src_ref=stiff_own,
                 dst_ref=stiff_r.at[k],
-                send_sem=stiff_send.at[k],
-                recv_sem=stiff_recv.at[k],
+                send_sem=stiff_sem.at[0],
+                recv_sem=stiff_sem.at[1],
                 device_id=along(k // 2, 1 - 2 * (k % 2)),
                 device_id_type=MESH,
             )
@@ -299,7 +311,7 @@
             load("prior", prior, modes)
         pack(0, c, field)
         if c == 0:
-            pl.semaphore_wait(barrier, nx + ny + nz - 3)
+            pl.semaphore_wait(barrier, 6)
             for copy in stiff_copies():
                 copy.start()
         for copy in face_copies(0, c):
@@ -365,14 +377,7 @@
         at = pl.ds(pl.multiple_of(VECS + 16 * g, 16), 16)
         place(at, [modes[16 * g + j].astype(F32) for j in range(16)])
 
-    rows_writes = [
-        pltpu.make_async_copy(whole.at[part], rows_out.at[part], rows_sem.at[k])
-        for k, part in enumerate([pl.ds(VECS, PRIOR), pl.ds(0, VECS)])
-    ]
-    rows_writes[0].start()
-
-    for copy in stiff_copies():
-        copy.wait_recv()
+    arrived(stiff_r, stiff_sem.at[1])
     around = jnp.concatenate(
         [stiff_own[...]]
         + [stiff_r[k] for k in range(4)]
@@ -386,7 +391,7 @@
     def operate(app, c, source, finish):
         slot = lax.rem(side((ROWS, LANES), 1), SLOT)
         joined = jnp.where(
-            slot < 3, low_z_r[app, c].astype(F32), high_z_r[app, c].astype(F32)
+            slot < 3, ends_r[app, c, 0].astype(F32), ends_r[app, c, 1].astype(F32)
         )
         cells = [source[c * CHUNK + j] for j in range(CHUNK)]
         lines = []
@@ -403,10 +408,10 @@
             rows = jnp.concatenate(
                 [
                     jnp.concatenate(cells[2 * p : 2 * p + 2], axis=1),
-                    high_x_r[app, c, 16 * p : 16 * p + 16],
-                    high_y_r[app, c, 16 * p : 16 * p + 16],
-                    low_x_r[app, c, 48 * q : 48 * q + 48],
-                    low_y_r[app, c, 48 * q : 48 * q + 48],
+                    faces_r[app, c, HIGH_X_R + 16 * p : HIGH_X_R + 16 * p + 16],
+                    faces_r[app, c, HIGH_Y_R + 16 * p : HIGH_Y_R + 16 * p + 16],
+                    faces_r[app, c, LOW_X_R + 48 * q : LOW_X_R + 48 * q + 48],
+                    faces_r[app, c, LOW_Y_R + 48 * q : LOW_Y_R + 48 * q + 48],
                     jnp.zeros((BLOCK - 192, 2 * LANES), BF16),
                 ],
                 axis=0,
@@ -435,8 +440,7 @@
 
     @pl.loop(0, CHUNKS)
     def _(c):
-        for copy in face_copies(0, c):
-            copy.wait_recv()
+        faces_arrived(0, c)
         operate(0, c, field, finish_one)
         pack(1, c, once)
         for copy in face_copies(1, c):
@@ -446,13 +450,16 @@
     def _(g):
         for k in range(16 // CHUNK):
             c = g * (16 // CHUNK) + k
-            for copy in face_copies(1, c):
-                copy.wait_recv()
+            faces_arrived(1, c)
+            if k == 0:
+                @pl.when(g == 0)
+                def _():
+                    greet(token.at[0])
+
             operate(1, c, once, finish_two)
         at = pl.ds(pl.multiple_of(16 * g, 16), 16)
         place(at, [image_rows[j] for j in range(16)])
 
-    rows_writes[1].start()
     sums = dot_nt(whole[:VECS], whole[...])
     sums = jnp.concatenate([sums, jnp.zeros((VECS, LANES - VECS - PRIOR), F32)], axis=1)
 
@@ -466,58 +473,39 @@
         ],
         axis=0,
     )
-    sent = []
+    pl.semaphore_wait(token.at[0], 6)
     for stage, (axis, slots) in enumerate(((2, slots_z), (0, slots_x), (1, slots_y))):
-        slots[me[axis]] = mine
-        here = slots.at[me[axis]]
-        copies = [
+        size = sizes[axis]
+        slots[0] = mine
+        steps = sorted(range(1, size), key=lambda step: -min(step, size - step))
+        for step in steps:
             pltpu.make_async_remote_copy(
-                src_ref=here,
-                dst_ref=here,
-                send_sem=sum_send.at[stage, step],
-                recv_sem=sum_recv.at[stage, step],
+                src_ref=slots.at[0],
+                dst_ref=slots.at[step],
+                send_sem=sum_send.at[stage],
+                recv_sem=sum_recv.at[stage],
                 device_id=along(axis, step),
                 device_id_type=MESH,
-            )
-            for step in range(1, sizes[axis])
-        ]
-        for copy in copies:
-            copy.start()
-        for copy in copies:
-            copy.wait_recv()
-        sent += copies
-        mine = slots[0]
-        for k in range(1, sizes[axis]):
-            mine = mine + slots[k]
+            ).start()
+        arrived(slots.at[pl.ds(1, size - 1)], sum_recv.at[stage])
+        parts = [slots[lax.rem(me[axis] - k + size, size)] for k in range(size)]
+        mine = parts[0]
+        for part in parts[1:]:
+            mine = mine + part
     tail = jnp.zeros((8, LANES), F32)
     for r in range(3):
         part = pltpu.roll(mine[8 * r : 8 * r + 8], LANES - used + 32 * r, 1)
         tail = jnp.where((lane >= 32 * r) & (lane < 32 * r + 32), part, tail)
     sums_out[...] = jnp.concatenate([mine, tail], axis=0)
 
-    for copy in sent + stiff_copies():
-        copy.wait_send()
-
-    @pl.loop(0, CHUNKS)
-    def _(c):
-        for app in range(2):
-            for copy in face_copies(app, c):
-                copy.wait_send()
-
-    for write in rows_writes:
-        write.wait()
-
-
-def finish_kernel(nodes_total, rows_in, sums_in, out, upper, whole, result, rows_sem, out_sem):
-    width = 2 * SIDE * LANES
-    parts = SIDE // 2
-    loads = []
-    for k in range(parts):
-        part = pl.ds(k * width, width)
-        load = pltpu.make_async_copy(rows_in.at[:, part], whole.at[:, part], rows_sem.at[k])
-        load.start()
-        loads.append(load)
-
+    for k, buffer in enumerate([low_x_s, high_x_s, low_y_s, high_y_s, ends_s, ends_s]):
+        arrived(buffer, send_sem.at[k])
+    arrived(stiff_r, stiff_sem.at[0])
+    for stage, slots in enumerate((slots_z, slots_x, slots_y)):
+        arrived(slots.at[pl.ds(1, slots.shape[0] - 1)], sum_send.at[stage])
+
+
+def finish_kernel(nodes_total, whole, sums_in, out, upper_out, result, upper, out_sem):
     lane = side((VECS, LANES), 1)
     line = side((VECS, LANES), 0)
     sums = sums_in[...] * (1.0 / nodes_total)
@@ -566,14 +554,14 @@
     diagonal = jnp.sum(jnp.where(lane == line, state, 0.0), axis=1, keepdims=True)
     state = state * (1.0 / jnp.sqrt(diagonal))
     upper[...] = jnp.where(lane >= line, state, 0.0)[:, :VECS]
+    writes = [pltpu.make_async_copy(upper, upper_out, out_sem.at[0])]
+    writes[0].start()
 
     solve = pltpu.roll(state, LANES - VECS, 1)[:, : VECS + PRIOR]
     high = solve.astype(BF16)
     low = (solve - high.astype(F32)).astype(BF16)
     solve = jnp.concatenate([high, low], axis=0)
-    writes = []
-    for k in range(parts):
-        loads[k].wait()
+    for k in range(SIDE // 2):
         blocks = []
         for x in (2 * k, 2 * k + 1):
             block = dot(solve, whole[:, x * SIDE * LANES : (x + 1) * SIDE * LANES])
@@ -586,7 +574,7 @@
         for v in range(VECS):
             result[v, at] = jnp.concatenate([blocks[0][v], blocks[1][v]], axis=0).astype(BF16)
         part = pl.ds(2 * k * SIDE, 2 * SIDE)
-        write = pltpu.make_async_copy(result.at[:, part], out.at[:, part], out_sem.at[k])
+        write = pltpu.make_async_copy(result.at[:, part], out.at[:, part], out_sem.at[1 + k])
         write.start()
         writes.append(write)
     for write in writes:
@@ -598,8 +586,8 @@
     tables = make_tables()
     low = (2, CHUNKS, 24 * PAIRS, 2 * LANES)
     high = (2, CHUNKS, 16 * PAIRS, 2 * LANES)
-    flat = (2, CHUNKS, ROWS, LANES)
-    any_space = pl.BlockSpec(memory_space=pl.ANY)
+    hbm = pl.BlockSpec(memory_space=pltpu.HBM)
+    vmem = pl.BlockSpec(memory_space=pltpu.VMEM)
     dma = pltpu.SemaphoreType.DMA
     rows, sums = pl.pallas_call(
         functools.partial(kernel, sizes, nodes_total),
@@ -607,8 +595,8 @@
             jax.ShapeDtypeStruct((VECS + PRIOR, ROWS * LANES), BF16),
             jax.ShapeDtypeStruct((VECS, LANES), F32),
         ),
-        in_specs=[any_space] * (4 + TABLES),
-        out_specs=(any_space, pl.BlockSpec(memory_space=pltpu.VMEM)),
+        in_specs=[hbm] * (4 + TABLES),
+        out_specs=(vmem, vmem),
         scratch_shapes=[pltpu.VMEM(t.shape, t.dtype) for t in tables]
         + [
             pltpu.VMEM((VECS, ROWS, LANES), BF16),
@@ -617,21 +605,16 @@
             pltpu.VMEM((ROWS, LANES), BF16),
             pltpu.VMEM((VECS, ROWS, LANES), BF16),
             pltpu.VMEM(low, BF16),
-            pltpu.VMEM(high, BF16),
             pltpu.VMEM(low, BF16),
             pltpu.VMEM(high, BF16),
-            pltpu.VMEM(flat, BF16),
-            pltpu.VMEM(low, BF16),
             pltpu.VMEM(high, BF16),
-            pltpu.VMEM(low, BF16),
-            pltpu.VMEM(high, BF16),
-            pltpu.VMEM(flat, BF16),
-            pltpu.VMEM(flat, BF16),
+            pltpu.VMEM((2, CHUNKS, ROWS, LANES), BF16),
+            pltpu.VMEM((2, CHUNKS, 80 * PAIRS, 2 * LANES), BF16),
+            pltpu.VMEM((2, CHUNKS, 2, ROWS, LANES), BF16),
             pltpu.VMEM((6, ROWS, LANES), BF16),
             pltpu.VMEM((BLOCK, LANES), F32),
             pltpu.VMEM((ROWS, BLOCK), F32),
             pltpu.VMEM((ROWS, LANES), F32),
-            pltpu.VMEM((VECS + PRIOR, ROWS * LANES), BF16),
             pltpu.VMEM((16, ROWS, LANES), F32),
             pltpu.VMEM((PAIRS, BLOCK, 2 * LANES), BF16),
             pltpu.VMEM((CHUNK * ROWS, BLOCK), BF16),
@@ -639,23 +622,27 @@
             pltpu.VMEM((nx, 24, LANES), F32),
             pltpu.VMEM((ny, 24, LANES), F32),
             dma((3 + CHUNKS + TABLES,)),
+            dma((6,)),
+            dma((2, CHUNKS, 2)),
             dma((2,)),
-            dma((6,)),
-            dma((6,)),
-            dma((2, CHUNKS, 6)),
-            dma((2, CHUNKS, 6)),
-            dma((3, max(sizes))),
-            dma((3, max(sizes))),
+            dma((3,)),
+            dma((3,)),
+            pltpu.SemaphoreType.REGULAR((1,)),
         ],
         compiler_params=pltpu.CompilerParams(
-            collective_id=0, has_side_effects=True, vmem_limit_bytes=56 * 2**20
+            collective_id=0, has_side_effects=True, vmem_limit_bytes=24 * 2**20
         ),
     )(
-        panel_in.reshape(VECS, ROWS, LANES),
-        prior_modes.reshape(PRIOR, ROWS, LANES),
-        stiffness.reshape(ROWS, LANES),
-        mass_shift.reshape(ROWS, LANES),
-        *[jnp.asarray(t) for t in tables],
+        *[
+            pltpu.with_memory_space_constraint(operand, pltpu.HBM)
+            for operand in [
+                panel_in.reshape(VECS, ROWS, LANES),
+                prior_modes.reshape(PRIOR, ROWS, LANES),
+                stiffness.reshape(ROWS, LANES),
+                mass_shift.reshape(ROWS, LANES),
+            ]
+            + [jnp.asarray(t) for t in tables]
+        ]
     )
     basis, upper = pl.pallas_call(
         functools.partial(finish_kernel, nodes_total),
@@ -663,15 +650,14 @@
             jax.ShapeDtypeStruct((VECS, ROWS, LANES), BF16),
             jax.ShapeDtypeStruct((VECS, VECS), F32),
         ),
-        in_specs=[any_space, pl.BlockSpec(memory_space=pltpu.VMEM)],
-        out_specs=(any_space, pl.BlockSpec(memory_space=pltpu.VMEM)),
+        in_specs=[vmem, vmem],
+        out_specs=(hbm, hbm),
         scratch_shapes=[
-            pltpu.VMEM((VECS + PRIOR, ROWS * LANES), BF16),
             pltpu.VMEM((VECS, ROWS, LANES), BF16),
-            dma((SIDE // 2,)),
-            dma((SIDE // 2,)),
+            pltpu.VMEM((VECS, VECS), F32),
+            dma((1 + SIDE // 2,)),
         ],
-        compiler_params=pltpu.CompilerParams(vmem_limit_bytes=56 * 2**20),
+        compiler_params=pltpu.CompilerParams(vmem_limit_bytes=12 * 2**20),
     )(rows, sums)
     return basis.reshape(panel_in.shape), upper
 

time: 49.2 us -> 42.7 us (0.87)
  Pallas kernels: 48.3 us -> 41.9 us
    pallas_call x1, Pallas kernels: 43.3 us -> 39.6 us  [on_device(): pl.pallas_call(functools.partial(kernel, sizes, nodes_total), out_shape=(...]
    pallas_call x1, Pallas kernels: 4.97 us -> 2.37 us  [on_device(): pl.pallas_call(functools.partial(finish_kernel, nodes_total), out_shape=(...]
where the time goes in v4:
time: 42.7 us; the launch traced here: 42.6 us
  Pallas kernels  41.9 us (98%)
  between operations  0.64 us (1%)
    pallas_call x1, Pallas kernels, on_device(): pl.pallas_call(functools.partial(kernel, sizes, nodes_total), out_shape=(...  39.6 us
    pallas_call x1, Pallas kernels, on_device(): pl.pallas_call(functools.partial(finish_kernel, nodes_total), out_shape=(...  2.37 us

profile of v4, /device:TPU:1, one launch (start us, length us, event | category | flops | bytes accessed | tf_op | source)
XLA Modules:
  0.0 42.6 jit_solution(7027599846461477681)
XLA Ops:
  0.6 39.6 %shard_map.149 = (bf16[96,8192]{1,0:T(8,128)(2,1)S(1)}, f32[32,128]{1,0:T(8,128)S(1)}) custom-call(bf16[32,64,128]{2,1,0:T(8,128)(2,1)} %bitcast.6, bf16[64,64,128]{2,1,0:T(8,128)(2,1)} %bitcast.5, bf16[64,128]{1,0:T(8,128)(2,1)} %bitcast.7, bf16[64,128]{1,0:T(8,128)(2,1)} %bitcast.8, bf16[2,256,256]{2,1,0:T(8,128)(2,1)} %constant.20.clone.refs_4_, ...), custom_call_target="tpu_custom_call" | custom-call | tf_op jit(solution)/shard_map/pallas_call | solution.py:592
  40.2 2.4 %shard_map.150 = (bf16[32,64,128]{2,1,0:T(8,128)(2,1)}, f32[32,32]{1,0:T(8,128)}) custom-call(bf16[96,8192]{1,0:T(8,128)(2,1)S(1)} %get-tuple-element.6.whole, f32[32,128]{1,0:T(8,128)S(1)} %get-tuple-element.7.sums_in), custom_call_target="tpu_custom_call" | custom-call | tf_op jit(solution)/shard_map/pallas_call | solution.py:647

commit v5 on v4

--- a/solution.py
+++ b/solution.py
@@ -20,7 +20,7 @@
 SIDE = 8
 ROWS = SIDE * SIDE
 LANES = 128
-CHUNK = 8
+CHUNK = 4
 CHUNKS = VECS // CHUNK
 PAIRS = CHUNK // 2
 SLOT = LANES // CHUNK
@@ -50,7 +50,9 @@
 
 HIGH_X, HIGH_Y, LOW_X, LOW_Y = 64, 80, 96, 144
 BLOCK = 256
-LOW_X_R, LOW_Y_R, HIGH_X_R, HIGH_Y_R = 0, 96, 192, 256
+LOW_X_R, LOW_Y_R, HIGH_Y_R = 0, 24 * PAIRS, 48 * PAIRS
+LOW_Z_R, HIGH_Z_R, HIGH_X_R = 64 * PAIRS, 64 * PAIRS + 32, 64 * PAIRS + 64
+FACE_ROWS = HIGH_X_R + 16 * PAIRS
 
 
 def field_row(x, y, parity):
@@ -176,13 +178,8 @@
         stiff_own,
         mass_own,
         once,
-        low_x_s,
-        low_y_s,
-        high_x_s,
-        high_y_s,
-        ends_s,
+        faces_s,
         faces_r,
-        ends_r,
         stiff_r,
         factor,
         factor_z,
@@ -240,41 +237,60 @@
             jnp.concatenate([cells[2 * p], cells[2 * p + 1]], axis=1) for p in range(PAIRS)
         ]
         for p in range(PAIRS):
-            high_x_s[app, c, 16 * p : 16 * p + 16] = pairs[p][:16]
+            at = HIGH_X_R + 16 * p
+            faces_s[app, c, at : at + 16] = pairs[p][:16]
         for q in range(PAIRS // 2):
             both = jnp.concatenate([pairs[2 * q], pairs[2 * q + 1]], axis=0)
             picked = dot(faces[...], both).astype(BF16)
-            high_y_s[app, c, 32 * q : 32 * q + 32] = picked[:32]
-            low_x_s[app, c, 48 * q : 48 * q + 48] = picked[32:80]
-            low_y_s[app, c, 48 * q : 48 * q + 48] = picked[80:]
+            for at, rows in (
+                (HIGH_Y_R + 32 * q, picked[:32]),
+                (LOW_X_R + 48 * q, picked[32:80]),
+                (LOW_Y_R + 48 * q, picked[80:]),
+            ):
+                faces_s[app, c, at : at + rows.shape[0]] = rows
         lane = side((ROWS, LANES), 1)
         edges = jnp.zeros((ROWS, LANES), F32)
         for j in range(CHUNK):
             here = (lane >= SLOT * j) & (lane < SLOT * j + 5)
             edges = jnp.where(here, pltpu.roll(cells[j].astype(F32), SLOT * j + 3, 1), edges)
-        ends_s[app, c] = edges.astype(BF16)
+        edges = edges.astype(BF16)
+        faces_s[app, c, LOW_Z_R : LOW_Z_R + 32] = jnp.concatenate(
+            [edges[:32], edges[32:]], axis=1
+        )
+
+    first = [me[k] == 0 for k in range(3)]
+    last = [me[k] == sizes[k] - 1 for k in range(3)]
+
+    def one_of(condition, yes, no):
+        return jnp.where(condition, yes, no).astype(jnp.int32)
+
+    def crosses(axis, step):
+        if axis != 0:
+            return False
+        return last[0] if step == 1 else first[0]
 
     def face_copies(app, c):
         plan = [
-            (low_x_s, LOW_X_R, 0, 1),
-            (high_x_s, HIGH_X_R, 0, -1),
-            (low_y_s, LOW_Y_R, 1, 1),
-            (high_y_s, HIGH_Y_R, 1, -1),
-            (ends_s, 0, 2, 1),
-            (ends_s, 1, 2, -1),
+            (LOW_X_R, LOW_X_R, 24 * PAIRS, 0, 1),
+            (HIGH_X_R, HIGH_X_R, 16 * PAIRS, 0, -1),
+            (LOW_Y_R, LOW_Y_R, 24 * PAIRS, 1, 1),
+            (HIGH_Y_R, HIGH_Y_R, 16 * PAIRS, 1, -1),
+            (LOW_Z_R, LOW_Z_R, 32, 2, 1),
+            (LOW_Z_R, HIGH_Z_R, 32, 2, -1),
         ]
         copies = []
-        for k, (src, at, axis, step) in enumerate(plan):
-            if axis == 2:
-                target = ends_r.at[app, c, at]
-            else:
-                target = faces_r.at[app, c, pl.ds(at, src.shape[2])]
+        for here, there, rows, axis, step in plan:
+            layer, signal = app, app * CHUNKS + c
+            if axis == 0:
+                aside = crosses(axis, step)
+                layer = one_of(aside, app + 2, app)
+                signal = one_of(aside, 2 * CHUNKS + (step < 0), signal)
             copies.append(
                 pltpu.make_async_remote_copy(
-                    src_ref=src.at[app, c],
-                    dst_ref=target,
-                    send_sem=send_sem.at[k],
-                    recv_sem=recv_sem.at[app, c, axis // 2],
+                    src_ref=faces_s.at[app, c, pl.ds(here, rows)],
+                    dst_ref=faces_r.at[layer, c, pl.ds(there, rows)],
+                    send_sem=send_sem.at[0],
+                    recv_sem=recv_sem.at[signal],
                     device_id=along(axis, step),
                     device_id_type=MESH,
                 )
@@ -284,22 +300,45 @@
     def arrived(buffer, semaphore):
         pltpu.make_async_copy(buffer, buffer, semaphore).wait()
 
+    inside = jnp.logical_not(first[0] | last[0])
+
+    def arrived_inside(buffer, low, high, semaphore):
+        rows = buffer.shape[0]
+        for condition, start, end in (
+            (inside, 0, rows),
+            (first[0], low, rows),
+            (last[0], 0, rows - high),
+        ):
+
+            @pl.when(condition)
+            def _(start=start, end=end):
+                arrived(buffer.at[pl.ds(start, end - start)], semaphore)
+
     def faces_arrived(app, c):
-        arrived(faces_r.at[app, c], recv_sem.at[app, c, 0])
-        arrived(ends_r.at[app, c], recv_sem.at[app, c, 1])
+        arrived_inside(
+            faces_r.at[app, c], 24 * PAIRS, 16 * PAIRS, recv_sem.at[app * CHUNKS + c]
+        )
 
     def stiff_copies():
-        return [
-            pltpu.make_async_remote_copy(
-                src_ref=stiff_own,
-                dst_ref=stiff_r.at[k],
-                send_sem=stiff_sem.at[0],
-                recv_sem=stiff_sem.at[1],
-                device_id=along(k // 2, 1 - 2 * (k % 2)),
-                device_id_type=MESH,
+        copies = []
+        for k, (axis, step) in enumerate(
+            [(0, 1), (1, 1), (1, -1), (2, 1), (2, -1), (0, -1)]
+        ):
+            slot, signal = k, 1
+            if axis == 0:
+                aside = crosses(axis, step)
+                slot, signal = one_of(aside, 6 + (step < 0), k), one_of(aside, 2, 1)
+            copies.append(
+                pltpu.make_async_remote_copy(
+                    src_ref=stiff_own,
+                    dst_ref=stiff_r.at[slot],
+                    send_sem=stiff_sem.at[0],
+                    recv_sem=stiff_sem.at[signal],
+                    device_id=along(axis, step),
+                    device_id_type=MESH,
+                )
             )
-            for k in range(6)
-        ]
+        return copies
 
     loaded("faces", "stiff")
     for c in range(CHUNKS):
@@ -312,6 +351,7 @@
         pack(0, c, field)
         if c == 0:
             pl.semaphore_wait(barrier, 6)
+            greet(token.at[0])
             for copy in stiff_copies():
                 copy.start()
         for copy in face_copies(0, c):
@@ -319,8 +359,19 @@
 
     loaded("table0", "table2", "table3", "table5")
 
-    first = [me[k] == 0 for k in range(3)]
-    last = [me[k] == sizes[k] - 1 for k in range(3)]
+    @pl.when(first[0])
+    def _():
+        stiff_r[0] = jnp.zeros((ROWS, LANES), BF16)
+        for app in range(2):
+            for c in range(CHUNKS):
+                faces_r[app, c, :LOW_Y_R] = jnp.zeros((LOW_Y_R, 2 * LANES), BF16)
+
+    @pl.when(last[0])
+    def _():
+        stiff_r[5] = jnp.zeros((ROWS, LANES), BF16)
+        for app in range(2):
+            for c in range(CHUNKS):
+                faces_r[app, c, HIGH_X_R:] = jnp.zeros((16 * PAIRS, 2 * LANES), BF16)
 
     def outside(index, spans):
         cut = index < 0
@@ -377,86 +428,108 @@
         at = pl.ds(pl.multiple_of(VECS + 16 * g, 16), 16)
         place(at, [modes[16 * g + j].astype(F32) for j in range(16)])
 
-    arrived(stiff_r, stiff_sem.at[1])
+    arrived_inside(stiff_r.at[pl.ds(0, 6)], 1, 1, stiff_sem.at[1])
     around = jnp.concatenate(
         [stiff_own[...]]
-        + [stiff_r[k] for k in range(4)]
+        + [stiff_r[k] for k in (0, 5, 1, 2)]
         + [jnp.zeros((STIFF_K - 5 * ROWS, LANES), BF16)],
         axis=0,
     )
     factor[...] = dot(pick[...], around) * scale[...]
-    around = jnp.concatenate([stiff_own[...], stiff_r[4], stiff_r[5]], axis=1)
+    around = jnp.concatenate([stiff_own[...], stiff_r[3], stiff_r[4]], axis=1)
     factor_z[...] = dot(around, pick_z[...]) * scale_z[...]
 
-    def operate(app, c, source, finish):
-        slot = lax.rem(side((ROWS, LANES), 1), SLOT)
-        joined = jnp.where(
-            slot < 3, ends_r[app, c, 0].astype(F32), ends_r[app, c, 1].astype(F32)
-        )
+    def gradient(app, c, slot, source):
+        lane = lax.rem(side((ROWS, LANES), 1), SLOT)
+        ends = [faces_r[app, c, at : at + 32].astype(F32) for at in (LOW_Z_R, HIGH_Z_R)]
+        low, high = [
+            jnp.concatenate([end[:, :LANES], end[:, LANES:]], axis=0) for end in ends
+        ]
+        joined = jnp.where(lane < 3, low, high)
         cells = [source[c * CHUNK + j] for j in range(CHUNK)]
         lines = []
         for j in range(CHUNK):
             rolled = pltpu.roll(joined, LANES - SLOT * j, 1) if j else joined
             lines.append(jnp.concatenate([cells[j], rolled.astype(BF16)], axis=1))
         factor_rows = jnp.concatenate([factor_z[...]] * CHUNK, axis=0)
-        flux_z[...] = (
+        flux_z[slot] = (
             dot(jnp.concatenate(lines, axis=0), grad_z[...]) * factor_rows
         ).astype(BF16)
         factor_two = jnp.concatenate([factor[...], factor[...]], axis=1)
         for p in range(PAIRS):
             q, parity = p // 2, p % 2
+
+            def face(at, rows):
+                return faces_r[app, c, at : at + rows]
+
             rows = jnp.concatenate(
                 [
                     jnp.concatenate(cells[2 * p : 2 * p + 2], axis=1),
-                    faces_r[app, c, HIGH_X_R + 16 * p : HIGH_X_R + 16 * p + 16],
-                    faces_r[app, c, HIGH_Y_R + 16 * p : HIGH_Y_R + 16 * p + 16],
-                    faces_r[app, c, LOW_X_R + 48 * q : LOW_X_R + 48 * q + 48],
-                    faces_r[app, c, LOW_Y_R + 48 * q : LOW_Y_R + 48 * q + 48],
+                    face(HIGH_X_R + 16 * p, 16),
+                    face(HIGH_Y_R + 16 * p, 16),
+                    face(LOW_X_R + 48 * q, 48),
+                    face(LOW_Y_R + 48 * q, 48),
                     jnp.zeros((BLOCK - 192, 2 * LANES), BF16),
                 ],
                 axis=0,
             )
-            flux[p] = (dot(grad[parity], rows) * factor_two).astype(BF16)
-        image_z = dot(flux_z[...], back_z[...])
+            flux[slot, p] = (dot(grad[parity], rows) * factor_two).astype(BF16)
+
+    def divergence(c, slot, source, finish):
+        image_z = dot(flux_z[slot], back_z[...])
         for p in range(PAIRS):
-            image = dot(back[...], flux[p])
-            moved = [
-                image[:, h * LANES : (h + 1) * LANES]
-                + image_z[(2 * p + h) * ROWS : (2 * p + h + 1) * ROWS]
-                - shift[...] * cells[2 * p + h].astype(F32)
-                for h in range(2)
-            ]
-            finish(c, p, moved)
-
-    def finish_one(c, p, moved):
-        for h in range(2):
-            once[c * CHUNK + 2 * p + h] = (moved[h] * (1.0 / filter_half)).astype(BF16)
-
-    def finish_two(c, p, moved):
-        for h in range(2):
-            j = c * CHUNK + 2 * p + h
-            done = moved[h] * (2.0 / filter_half) - field[j].astype(F32)
-            image_rows[lax.rem(j, 16)] = done
-
-    @pl.loop(0, CHUNKS)
-    def _(c):
-        faces_arrived(0, c)
-        operate(0, c, field, finish_one)
+            image = dot(back[...], flux[slot, p])
+            for h in range(2):
+                j = 2 * p + h
+                cell = source[c * CHUNK + j].astype(F32)
+                moved = image[:, h * LANES : (h + 1) * LANES]
+                moved = moved + image_z[j * ROWS : (j + 1) * ROWS] - shift[...] * cell
+                finish(c * CHUNK + j, moved)
+
+    def finish_one(j, moved):
+        once[j] = (moved * (1.0 / filter_half)).astype(BF16)
+
+    def finish_two(j, moved):
+        done = moved * (2.0 / filter_half) - field[j].astype(F32)
+        image_rows[lax.rem(j, 16)] = done
+
+    group = 16 // CHUNK
+
+    def send_once(c):
         pack(1, c, once)
         for copy in face_copies(1, c):
             copy.start()
 
-    @pl.loop(0, VECS // 16)
+    pl.semaphore_wait(token.at[0], 6)
+    greet(token.at[1])
+
+    @pl.loop(0, CHUNKS // group)
     def _(g):
-        for k in range(16 // CHUNK):
-            c = g * (16 // CHUNK) + k
+        for k in range(group):
+            c = g * group + k
+            faces_arrived(0, c)
+            if k > 0:
+                divergence(c - 1, (k - 1) % 2, field, finish_one)
+            gradient(0, c, k % 2, field)
+            if k > 0:
+                send_once(c - 1)
+        c = g * group + group - 1
+        divergence(c, (group - 1) % 2, field, finish_one)
+        send_once(c)
+
+    pl.semaphore_wait(token.at[1], 6)
+    greet(token.at[2])
+
+    @pl.loop(0, CHUNKS // group)
+    def _(g):
+        for k in range(group):
+            c = g * group + k
             faces_arrived(1, c)
-            if k == 0:
-                @pl.when(g == 0)
-                def _():
-                    greet(token.at[0])
-
-            operate(1, c, once, finish_two)
+            if k > 0:
+                divergence(c - 1, (k - 1) % 2, once, finish_two)
+            gradient(1, c, k % 2, once)
+        c = g * group + group - 1
+        divergence(c, (group - 1) % 2, once, finish_two)
         at = pl.ds(pl.multiple_of(16 * g, 16), 16)
         place(at, [image_rows[j] for j in range(16)])
 
@@ -473,7 +546,7 @@
         ],
         axis=0,
     )
-    pl.semaphore_wait(token.at[0], 6)
+    pl.semaphore_wait(token.at[2], 6)
     for stage, (axis, slots) in enumerate(((2, slots_z), (0, slots_x), (1, slots_y))):
         size = sizes[axis]
         slots[0] = mine
@@ -498,9 +571,22 @@
         tail = jnp.where((lane >= 32 * r) & (lane < 32 * r + 32), part, tail)
     sums_out[...] = jnp.concatenate([mine, tail], axis=0)
 
-    for k, buffer in enumerate([low_x_s, high_x_s, low_y_s, high_y_s, ends_s, ends_s]):
-        arrived(buffer, send_sem.at[k])
-    arrived(stiff_r, stiff_sem.at[0])
+    arrived(faces_r.at[pl.ds(0, 2)], send_sem.at[0])
+    arrived(stiff_r.at[pl.ds(0, 6)], stiff_sem.at[0])
+
+    @pl.when(first[0])
+    def _():
+        arrived(faces_r.at[pl.ds(2, 2), :, pl.ds(0, LOW_Y_R)], recv_sem.at[2 * CHUNKS])
+        arrived(stiff_r.at[6], stiff_sem.at[2])
+
+    @pl.when(last[0])
+    def _():
+        arrived(
+            faces_r.at[pl.ds(2, 2), :, pl.ds(HIGH_X_R, 16 * PAIRS)],
+            recv_sem.at[2 * CHUNKS + 1],
+        )
+        arrived(stiff_r.at[7], stiff_sem.at[2])
+
     for stage, slots in enumerate((slots_z, slots_x, slots_y)):
         arrived(slots.at[pl.ds(1, slots.shape[0] - 1)], sum_send.at[stage])
 
@@ -584,8 +670,6 @@
 def on_device(sizes, nodes_total, panel_in, prior_modes, stiffness, mass_shift):
     nx, ny, nz = sizes
     tables = make_tables()
-    low = (2, CHUNKS, 24 * PAIRS, 2 * LANES)
-    high = (2, CHUNKS, 16 * PAIRS, 2 * LANES)
     hbm = pl.BlockSpec(memory_space=pltpu.HBM)
     vmem = pl.BlockSpec(memory_space=pltpu.VMEM)
     dma = pltpu.SemaphoreType.DMA
@@ -604,30 +688,25 @@
             pltpu.VMEM((ROWS, LANES), BF16),
             pltpu.VMEM((ROWS, LANES), BF16),
             pltpu.VMEM((VECS, ROWS, LANES), BF16),
-            pltpu.VMEM(low, BF16),
-            pltpu.VMEM(low, BF16),
-            pltpu.VMEM(high, BF16),
-            pltpu.VMEM(high, BF16),
-            pltpu.VMEM((2, CHUNKS, ROWS, LANES), BF16),
-            pltpu.VMEM((2, CHUNKS, 80 * PAIRS, 2 * LANES), BF16),
-            pltpu.VMEM((2, CHUNKS, 2, ROWS, LANES), BF16),
-            pltpu.VMEM((6, ROWS, LANES), BF16),
+            pltpu.VMEM((2, CHUNKS, FACE_ROWS, 2 * LANES), BF16),
+            pltpu.VMEM((4, CHUNKS, FACE_ROWS, 2 * LANES), BF16),
+            pltpu.VMEM((8, ROWS, LANES), BF16),
             pltpu.VMEM((BLOCK, LANES), F32),
             pltpu.VMEM((ROWS, BLOCK), F32),
             pltpu.VMEM((ROWS, LANES), F32),
             pltpu.VMEM((16, ROWS, LANES), F32),
-            pltpu.VMEM((PAIRS, BLOCK, 2 * LANES), BF16),
-            pltpu.VMEM((CHUNK * ROWS, BLOCK), BF16),
+            pltpu.VMEM((2, PAIRS, BLOCK, 2 * LANES), BF16),
+            pltpu.VMEM((2, CHUNK * ROWS, BLOCK), BF16),
             pltpu.VMEM((nz, 24, LANES), F32),
             pltpu.VMEM((nx, 24, LANES), F32),
             pltpu.VMEM((ny, 24, LANES), F32),
             dma((3 + CHUNKS + TABLES,)),
-            dma((6,)),
-            dma((2, CHUNKS, 2)),
-            dma((2,)),
+            dma((1,)),
+            dma((2 * CHUNKS + 2,)),
             dma((3,)),
             dma((3,)),
-            pltpu.SemaphoreType.REGULAR((1,)),
+            dma((3,)),
+            pltpu.SemaphoreType.REGULAR((3,)),
         ],
         compiler_params=pltpu.CompilerParams(
             collective_id=0, has_side_effects=True, vmem_limit_bytes=24 * 2**20

time: 42.7 us -> 42.7 us (level)
  no operation moved by 1% of the time
where the time goes in v5:
time: 42.7 us; the launch traced here: 42.5 us
  Pallas kernels  41.9 us (98%)
  between operations  0.64 us (1%)
    pallas_call x1, Pallas kernels, on_device(): pl.pallas_call(functools.partial(kernel, sizes, nodes_total), out_shape=(...  39.5 us
    pallas_call x1, Pallas kernels, on_device(): pl.pallas_call(functools.partial(finish_kernel, nodes_total), out_shape=(...  2.37 us

profile of v5, /device:TPU:1, one launch (start us, length us, event | category | flops | bytes accessed | tf_op | source)
XLA Modules:
  0.0 42.5 jit_solution(16148186109299262421)
XLA Ops:
  0.6 39.5 %shard_map.149 = (bf16[96,8192]{1,0:T(8,128)(2,1)S(1)}, f32[32,128]{1,0:T(8,128)S(1)}) custom-call(bf16[32,64,128]{2,1,0:T(8,128)(2,1)} %bitcast.6, bf16[64,64,128]{2,1,0:T(8,128)(2,1)} %bitcast.5, bf16[64,128]{1,0:T(8,128)(2,1)} %bitcast.7, bf16[64,128]{1,0:T(8,128)(2,1)} %bitcast.8, bf16[2,256,256]{2,1,0:T(8,128)(2,1)} %constant.20.clone.refs_4_, ...), custom_call_target="tpu_custom_call" | custom-call | tf_op jit(solution)/shard_map/pallas_call | solution.py:676
  40.2 2.4 %shard_map.150 = (bf16[32,64,128]{2,1,0:T(8,128)(2,1)}, f32[32,32]{1,0:T(8,128)}) custom-call(bf16[96,8192]{1,0:T(8,128)(2,1)S(1)} %get-tuple-element.6.whole, f32[32,128]{1,0:T(8,128)S(1)} %get-tuple-element.7.sums_in), custom_call_target="tpu_custom_call" | custom-call | tf_op jit(solution)/shard_map/pallas_call | solution.py:726
